TPU v7x, 32 devices: a whole 2x2x4 slice. The times are simulated.
32 devices in a mesh: groups: 2 (over x), tm: 16 (over z, y, core).
Axes of the slice: x: 2, y: 2, z: 4, core: 2. Of those that a mesh axis runs over, the one named last changes fastest.
Arguments:
- latent: bfloat16 [16384, 384], P(('groups', 'tm')), parts along dimension 0, may hold values from -45 to 45
- owner: int32 [16384], P(('groups', 'tm')), parts along dimension 0, may hold values from 0 to 15, as said below
- frame_counts: int32 [16], P('groups'), parts along dimension 0, may hold values from 1 to 8, 32 in all
- norm_gain: float32 [384], replicated, may hold values from 0.1 to 1.9
- norm_shift: float32 [384], replicated, may hold values from -3 to 3
- res_kernel: bfloat16 [3, 3, 3, 384, 384], replicated, may hold values from -0.0625 to 0.0625
- res_bias: float32 [384], replicated, may hold values from -3 to 3
- time_kernel: bfloat16 [3, 384, 768], replicated, may hold values from -0.1875 to 0.1875
- time_bias: float32 [768], replicated, may hold values from -3 to 3
- up_kernel: bfloat16 [3, 3, 384, 192], replicated, may hold values from -0.109375 to 0.109375
- up_bias: float32 [192], replicated, may hold values from -3 to 3
Outputs:
- frames_out: bfloat16 [128, 32, 6144], P(('groups', 'tm')), parts along dimension 0
There are 2 independent parts, one for each index of `groups`. A program takes and returns all parts, laid end to end along the dimension named above; an argument that names none is the same for every part. Nothing has to cross between parts.
Inputs may be any that keep to these rules, and one draw needn't show every extreme that they name: Each device's block of 512 tokens holds at most 64 tokens for any one owner, some block holds exactly 64 for one owner, and every device is the owner of exactly 512 tokens.
All inputs are finite; a program needn't handle non-finite values.
Results may differ from a plain program's by a relative error of at most 0.0057.
Values may be sent and summed in bfloat16 or wider, within the bound.
No kernel may reach another device: no remote copies, remote signals or barrier semaphores. Data moves between devices by JAX's collectives and lax.ppermute only.
A program may use at most 128 MiB of HBM per device.

v0:
```python
import functools

import jax
import jax.numpy as jnp
from jax import lax
from jax.experimental import pallas as pl
from jax.experimental.pallas import tpu as pltpu
from jax.sharding import PartitionSpec as P

H = 16
W = 16
MARK = 128.0
epsilon = 1e-06
MIB = 1 << 20
f32 = jnp.float32
bf16 = jnp.bfloat16


def in_vmem(value):
    return pltpu.with_memory_space_constraint(value, pltpu.VMEM)


VM = pl.BlockSpec(memory_space=pltpu.VMEM)
SM = pl.BlockSpec(memory_space=pltpu.SMEM)


def iota(shape, dim):
    return lax.broadcasted_iota(jnp.int32, shape, dim)


def mm(lhs, rhs):
    return jnp.dot(lhs, rhs, preferred_element_type=f32)


def from_behind(value, axis, by):
    size = lax.axis_size(axis)
    pairs = [(i, i + by) for i in range(size) if 0 <= i + by < size]
    return lax.ppermute(value, axis, pairs)


def pack_kernel(owner_ref, latent_ref, out_ref, *, peers, capacity):
    tokens = latent_ref.shape[0]
    owner = owner_ref[...]
    marked = iota((peers, tokens), 0) == owner
    upper = (iota((tokens, tokens), 0) <= iota((tokens, tokens), 1)).astype(bf16)
    running = mm(marked.astype(bf16), upper)
    rank = jnp.sum(jnp.where(marked, running - 1.0, 0.0), 0, keepdims=True)
    slot = owner * capacity + rank.astype(jnp.int32)
    chosen = (iota((peers * capacity, tokens), 0) == slot).astype(bf16)
    rows = mm(chosen, latent_ref[...])
    filled = mm(chosen, jnp.ones((tokens, 128), bf16))
    empty = jnp.concatenate([(1.0 - filled) * MARK] * (rows.shape[1] // 128), 1)
    out_ref[...] = (rows + empty).astype(bf16)


def unpack_kernel(
    got_ref, gain_ref, shift_ref, decoded_ref, active_ref, *, peers, capacity
):
    slots, channels = got_ref.shape
    tokens = decoded_ref.shape[0]
    present = (got_ref[:, :128] < MARK / 2).astype(bf16)
    slot_of = iota((peers, slots), 1)
    member = (slot_of // capacity == iota((peers, slots), 0)).astype(bf16)
    counts = mm(member, present)
    below = (iota((peers, peers), 1) < iota((peers, peers), 0)).astype(f32)
    before = jnp.dot(below, counts, precision=lax.Precision.HIGHEST, preferred_element_type=f32)
    member32 = member.astype(f32)
    first = jnp.sum(member32 * before[:, :1], 0, keepdims=True).astype(jnp.int32)
    held = jnp.sum(member32 * counts[:, :1], 0, keepdims=True).astype(jnp.int32)
    within = iota((1, slots), 1) % capacity
    place = jnp.where(within < held, first + within, -1)
    row = iota((tokens, slots), 0)
    pixel = row % (H * W)
    source = row - pixel + (pixel % H) * W + pixel // H
    chosen = (source == place).astype(bf16)
    values = mm(chosen, got_ref[...])
    decoded_ref[...] = values.astype(bf16)
    squares = jnp.mean(values * values, -1, keepdims=True)
    scaled = values * lax.rsqrt(squares + epsilon)
    fed = scaled * gain_ref[...] + shift_ref[...]
    active_ref[...] = (fed / (1.0 + jnp.exp(-fed))).astype(bf16)


def vertical(frame):
    wide = frame.astype(f32)
    y = iota(wide.shape, 0) % H
    up = jnp.where(y == 0, 0.0, pltpu.roll(wide, 1, 0))
    down = jnp.where(y == H - 1, 0.0, pltpu.roll(wide, wide.shape[0] - 1, 0))
    return up.astype(bf16), frame, down.astype(bf16)


def patches(frame, out_ref, first):
    pixels, channels = frame.shape
    nothing = jnp.zeros((H, channels), bf16)
    for a, shifted in enumerate(vertical(frame)):
        for b in range(3):
            if b == 0:
                moved = jnp.concatenate([nothing, shifted[: pixels - H]], 0)
            elif b == 1:
                moved = shifted
            else:
                moved = jnp.concatenate([shifted[H:], nothing], 0)
            at = (a * 3 + b) * channels
            out_ref[first : first + pixels, at : at + channels] = moved


def keeps(counts_ref, position_ref):
    first = position_ref[0] * 2
    starts = [jnp.int32(0), jnp.int32(0)]
    end = jnp.int32(0)
    for video in range(counts_ref.shape[0]):
        end = end + counts_ref[video]
        starts = [jnp.where(end <= first + f, end, starts[f]) for f in range(2)]
    return [
        [(first + f - back >= starts[f]).astype(f32) for back in range(3)] for f in range(2)
    ]


def local_conv_kernel(counts_ref, position_ref, active_ref, kernel_ref, out_ref, near):
    pixels = H * W
    keep = keeps(counts_ref, position_ref)
    for f in range(2):
        patches(active_ref[f * pixels : (f + 1) * pixels, :], near, f * pixels)
    own = mm(near[...], kernel_ref[2])
    out_ref[:pixels] = own[:pixels]
    out_ref[pixels:] = own[pixels:] + keep[1][1] * mm(near[:pixels], kernel_ref[1])


def residual_kernel(
    counts_ref, position_ref, prior_ref, kernel_ref, local_ref, decoded_ref, bias_ref, out_ref, near
):
    pixels = H * W
    keep = keeps(counts_ref, position_ref)
    for f in range(2):
        patches(prior_ref[f * pixels : (f + 1) * pixels, :], near, f * pixels)
    far = mm(near[...], kernel_ref[0])
    behind = mm(near[pixels:], kernel_ref[1])
    base = local_ref[...] + decoded_ref[...].astype(f32) + bias_ref[...]
    out_ref[:pixels] = (base[:pixels] + keep[0][2] * far[:pixels] + keep[0][1] * behind).astype(bf16)
    out_ref[pixels:] = (base[pixels:] + keep[1][2] * far[pixels:]).astype(bf16)


def local_time_kernel(counts_ref, position_ref, residual_ref, kernel_ref, bias_ref, out_ref):
    pixels = H * W
    keep = keeps(counts_ref, position_ref)
    own = mm(residual_ref[...], kernel_ref[2]) + bias_ref[...]
    out_ref[:pixels] = own[:pixels]
    out_ref[pixels:] = own[pixels:] + keep[1][1] * mm(residual_ref[:pixels], kernel_ref[1])


def up_kernel_body(
    counts_ref, position_ref, prior_ref, kernel_ref, local_ref, folded_ref, bias_ref, out_ref,
    near, rows32,
):
    pixels = H * W
    channels = prior_ref.shape[1]
    outs = bias_ref.shape[1]
    keep = keeps(counts_ref, position_ref)
    step = pl.program_id(0)

    @pl.when(step == 0)
    def _():
        far = mm(prior_ref[...], kernel_ref[0])
        behind = mm(prior_ref[pixels:], kernel_ref[1])
        first = local_ref[:pixels] + keep[0][2] * far[:pixels] + keep[0][1] * behind
        second = local_ref[pixels:] + keep[1][2] * far[pixels:]
        for f, wide in enumerate((first, second)):
            temporal = wide.astype(bf16)
            for half in range(2):
                e = 2 * f + half
                near[e, :H] = jnp.zeros((H, 3 * channels), bf16)
                near[e, H + pixels :] = jnp.zeros((H, 3 * channels), bf16)
                frame = temporal[:, half * channels : (half + 1) * channels]
                for a, shifted in enumerate(vertical(frame)):
                    near[e, H : H + pixels, a * channels : (a + 1) * channels] = shifted

    for p in range(2):
        phases = []
        for q in range(2):
            total = bias_ref[...] + jnp.zeros((pixels, outs), f32)
            for side in range(2):
                window = near[
                    step,
                    (q + side) * H : (q + side) * H + pixels,
                    p * channels : (p + 2) * channels,
                ]
                total = total + mm(window, folded_ref[q, side, p])
            phases.append(total)
        both = jnp.concatenate(phases, 1)
        blocks = 2 * outs // 128
        for x in range(W):
            for block in range(blocks):
                rows32[x * blocks + block, pl.ds(p, H, stride=2)] = both[
                    x * H : (x + 1) * H, block * 128 : (block + 1) * 128
                ]
    for block in range(rows32.shape[0]):
        out_ref[0, :, block * 128 : (block + 1) * 128] = rows32[block].astype(bf16)


def fold(up_kernel):
    taps = up_kernel.astype(f32)
    rows = jnp.stack(
        [jnp.stack([taps[0], taps[1] + taps[2]]), jnp.stack([taps[0] + taps[1], taps[2]])]
    )
    left = rows[:, :, 0], rows[:, :, 1] + rows[:, :, 2]
    right = rows[:, :, 0] + rows[:, :, 1], rows[:, :, 2]
    whole = jnp.stack([jnp.stack(left), jnp.stack(right)]).astype(bf16)
    return whole.reshape(2, 2, 2, 2 * taps.shape[2], taps.shape[3])


def on_device(
    latent,
    owner,
    frame_counts,
    norm_gain,
    norm_shift,
    res_kernel,
    res_bias,
    time_kernel,
    time_bias,
    up_kernel,
    up_bias,
):
    peers = lax.axis_size("tm")
    position = lax.axis_index("tm").astype(jnp.int32).reshape(1)
    tokens, channels = latent.shape
    capacity = 2 * tokens // peers
    pixels = H * W
    wide = time_kernel.shape[-1]
    outs = up_kernel.shape[-1]
    kernel = res_kernel.reshape(3, 9 * channels, channels)
    folded = fold(up_kernel)

    packed = pl.pallas_call(
        functools.partial(pack_kernel, peers=peers, capacity=capacity),
        out_shape=pltpu.VMEM((peers * capacity, channels), bf16),
        in_specs=[VM, VM],
        out_specs=VM,
        compiler_params=pltpu.CompilerParams(vmem_limit_bytes=16 * MIB),
        name="pack",
    )(owner.reshape(1, tokens), latent)
    received = lax.all_to_all(packed, "tm", split_axis=0, concat_axis=0, tiled=True)
    decoded, active = pl.pallas_call(
        functools.partial(unpack_kernel, peers=peers, capacity=capacity),
        out_shape=[pltpu.VMEM((tokens, channels), bf16)] * 2,
        in_specs=[VM] * 3,
        out_specs=[VM] * 2,
        compiler_params=pltpu.CompilerParams(vmem_limit_bytes=16 * MIB),
        name="unpack",
    )(in_vmem(received), norm_gain.reshape(1, channels), norm_shift.reshape(1, channels))
    prior = from_behind(active, "tm", 1)
    kernel = in_vmem(kernel)
    local = pl.pallas_call(
        local_conv_kernel,
        out_shape=pltpu.VMEM((tokens, channels), f32),
        in_specs=[SM, SM, VM, VM],
        out_specs=VM,
        scratch_shapes=[pltpu.VMEM((tokens, 9 * channels), bf16)],
        compiler_params=pltpu.CompilerParams(vmem_limit_bytes=16 * MIB),
        cost_estimate=pl.CostEstimate(
            flops=6 * pixels * 9 * channels * channels, bytes_accessed=0, transcendentals=0
        ),
        name="local_conv",
    )(frame_counts, position, in_vmem(active), kernel)
    residual = pl.pallas_call(
        residual_kernel,
        out_shape=pltpu.VMEM((tokens, channels), bf16),
        in_specs=[SM, SM] + [VM] * 5,
        out_specs=VM,
        scratch_shapes=[pltpu.VMEM((tokens, 9 * channels), bf16)],
        compiler_params=pltpu.CompilerParams(vmem_limit_bytes=16 * MIB),
        name="residual",
    )(
        frame_counts,
        position,
        in_vmem(prior),
        kernel,
        in_vmem(local),
        in_vmem(decoded),
        res_bias.reshape(1, channels),
    )
    prior_residual = from_behind(residual, "tm", 1)
    time_kernel = in_vmem(time_kernel)
    local_time = pl.pallas_call(
        local_time_kernel,
        out_shape=pltpu.VMEM((tokens, wide), f32),
        in_specs=[SM, SM] + [VM] * 3,
        out_specs=VM,
        compiler_params=pltpu.CompilerParams(vmem_limit_bytes=16 * MIB),
        cost_estimate=pl.CostEstimate(
            flops=6 * pixels * channels * wide, bytes_accessed=0, transcendentals=0
        ),
        name="local_time",
    )(frame_counts, position, in_vmem(residual), time_kernel, time_bias.reshape(1, wide))
    frames = 2 * tokens // pixels
    return pl.pallas_call(
        up_kernel_body,
        out_shape=jax.ShapeDtypeStruct((frames, 2 * H, 2 * W * outs), bf16),
        grid=(frames,),
        in_specs=[SM, SM] + [VM] * 5,
        out_specs=pl.BlockSpec((1, 2 * H, 2 * W * outs), lambda e: (e, 0, 0)),
        scratch_shapes=[
            pltpu.VMEM((frames, 2 * H + pixels, 3 * channels), bf16),
            pltpu.VMEM((2 * W * outs // 128, 2 * H, 128), f32),
        ],
        compiler_params=pltpu.CompilerParams(vmem_limit_bytes=20 * MIB),
        name="upscale",
    )(
        frame_counts,
        position,
        in_vmem(prior_residual),
        time_kernel,
        in_vmem(local_time),
        in_vmem(folded),
        up_bias.reshape(1, outs),
    )


def solution(mesh):
    placed = (
        P(("groups", "tm"), None),
        P(("groups", "tm")),
        P("groups"),
        P(),
        P(),
        P(),
        P(),
        P(),
        P(),
        P(),
        P(),
    )
    return jax.shard_map(
        on_device,
        mesh=mesh,
        in_specs=placed,
        out_specs=P(("groups", "tm"), None, None),
        check_vma=False,
    )
```

profile of v0, /device:TPU:0, one launch (start us, length us, event | category | flops | bytes accessed | tf_op | source)
XLA Modules:
  0.0 70.0 jit_solution(3797877027669258284)
XLA Ops:
  0.0 1.0 %copy-done.2 = bf16[512,384]{1,0:T(8,128)(2,1)S(1)} copy-done((bf16[512,384]{1,0:T(8,128)(2,1)S(1)}, bf16[512,384]{1,0:T(8,128)(2,1)}, u32[]{:S(2)}) %copy-start.2) | copy-done | bytes 393240
  1.0 0.7 copy-done.4
  1.7 2.0 %pack.1 = bf16[1024,384]{1,0:T(8,128)(2,1)} custom-call(s32[1,512]{1,0:T(1,128)S(1)} %bitcast.17, bf16[512,384]{1,0:T(8,128)(2,1)S(1)} %copy-done.2), custom_call_target="tpu_custom_call" | custom-call | tf_op jit(solution)/shard_map/pack/pallas_call | solution.py:234
  3.7 7.4 %all-to-all-start = ((bf16[16,64,384]{2,1,0:T(8,128)(2,1)}), bf16[16,64,384]{2,1,0:T(8,128)(2,1)S(1)}, u32[]{:S(2)}, u32[]{:S(2)}) async-start(bf16[16,64,384]{2,1,0:T(8,128)(2,1)} %bitcast.2), calls=%async_computation | async-start | bytes 1572864 | tf_op jit(solution)/shard_map/all_to_all | solution.py:242
  11.1 0.0 copy-start.9
  11.1 0.0 copy-start.10
  11.2 0.2 convert_element_type.5
  11.4 0.4 copy-done.9
  11.8 0.0 copy-done.10
  11.8 1.4 %fusion.4 = (f32[1,3,384,192]{2,3,1,0:T(8,128)}, f32[1,3,384,192]{2,3,1,0:T(8,128)}) fusion(bf16[3,3,384,192]{2,3,1,0:T(8,128)(2,1)S(1)} %copy-done.7), kind=kLoop, calls=%fused_computation.16 | loop fusion | bytes 3538944 | tf_op jit(solution)/shard_map/slice | solution.py:203
  13.2 1.3 %slice_add_fusion.1 = (f32[1,3,384,192]{2,3,1,0:T(8,128)}, f32[1,3,384,192]{2,3,1,0:T(8,128)}) fusion(f32[3,3,384,192]{2,3,1,0:T(8,128)S(1)} %convert_element_type.5), kind=kLoop, calls=%fused_computation.13 | loop fusion | flops 442368 | bytes 4423680 | tf_op jit(solution)/shard_map/add | solution.py:203
  14.5 15.3 %all-to-all-done = bf16[16,64,384]{2,1,0:T(8,128)(2,1)S(1)} async-done(((bf16[16,64,384]{2,1,0:T(8,128)(2,1)}), bf16[16,64,384]{2,1,0:T(8,128)(2,1)S(1)}, u32[]{:S(2)}, u32[]{:S(2)}) %all-to-all-start) | async-done | bytes 786464 | tf_op jit(solution)/shard_map/all_to_all | solution.py:242
  29.8 1.4 %unpack.1 = (bf16[512,384]{1,0:T(8,128)(2,1)S(1)}, bf16[512,384]{1,0:T(8,128)(2,1)S(1)}) custom-call(bf16[1024,384]{1,0:T(8,128)(2,1)S(1)} %bitcast.16, f32[1,384]{1,0:T(1,128)S(1)} %reshape.77.gain_ref, f32[1,384]{1,0:T(1,128)S(1)} %reshape.78.shift_ref), custom_call_target="tpu_custom_call" | custom-call | tf_op jit(solution)/shard_map/unpack/pallas_call | solution.py:243
  31.2 2.2 %collective-permute-start = (bf16[512,384]{1,0:T(8,128)(2,1)S(1)}, bf16[512,384]{1,0:T(8,128)(2,1)S(1)}, u32[]{:S(2)}, u32[]{:S(2)}) collective-permute-start(bf16[512,384]{1,0:T(8,128)(2,1)S(1)} %get-tuple-element.7.active_ref), channel_id=1, source_target_pairs={{0,1},{1,2},{2,3},{3,4},{4,5},{5,6},{6,7},{7,8},{8,9},{9,10},{10,1... | collective-permute-start | bytes 1179656 | tf_op jit(solution)/shard_map/ppermute | solution.py:38
  33.4 0.0 copy-start.11
  33.4 3.4 %maximum_bitcast_fusion = (f32[1,2,3,384,192]{3,4,2,1,0:T(8,128)S(1)}, f32[1,2,3,384,192]{3,4,2,1,0:T(8,128)}) fusion(f32[1,3,384,192]{2,3,1,0:T(8,128)} %get-tuple-element.13, f32[1,3,384,192]{2,3,1,0:T(8,128)} %get-tuple-element.15, f32[1,3,384,192]{2,3,1,0:T(8,128)} %get-tuple-element.16, f32[1,3,384,192]{2,3,1,0:T(8,128)} %get-tuple-element.14), kind=kLoop, calls=%fused_computation.5 | loop fusion | flops 884736 | bytes 7077888 | tf_op jit(solution)/shard_map/stack | solution.py:202
  36.9 2.8 %add_convert_fusion.1 = (bf16[2,2,1,384,192]{3,4,2,1,0:T(8,128)(2,1)}, bf16[2,2,1,384,192]{3,4,2,1,0:T(8,128)(2,1)S(1)}) fusion(f32[1,2,3,384,192]{3,4,2,1,0:T(8,128)} %get-tuple-element.18, f32[1,2,3,384,192]{3,4,2,1,0:T(8,128)S(1)} %get-tuple-element.17), kind=kLoop, calls=%fused_computation.11 | loop fusion | flops 2359296 | bytes 4718592 | tf_op jit(solution)/shard_map/convert.5
  39.6 3.3 %copy-done = bf16[3,3,3,384,384]{4,3,2,1,0:T(8,128)(2,1)S(1)} copy-done((bf16[3,3,3,384,384]{4,3,2,1,0:T(8,128)(2,1)S(1)}, bf16[3,3,3,384,384]{4,3,2,1,0:T(8,128)(2,1)}, u32[]{:S(2)}) %copy-start) | copy-done | bytes 7962648
  42.9 3.7 %local_conv.1.local_ref = f32[512,384]{1,0:T(8,128)S(1)} custom-call(s32[8]{0:T(128)S(1)} %copy-done.3, s32[1]{0:T(128)} %bitcast.position_ref, bf16[512,384]{1,0:T(8,128)(2,1)S(1)} %get-tuple-element.7.active_ref, bf16[3,3456,384]{2,1,0:T(8,128)(2,1)S(1)} %bitcast.14), custom_call_target="tpu_custom_call" | custom-call | flops 2038431744 | tf_op jit(solution)/shard_map/local_conv/pallas_call | solution.py:253
  46.6 0.0 collective-permute-done.prior_ref
  46.6 3.7 %residual.1.residual_ref = bf16[512,384]{1,0:T(8,128)(2,1)S(1)} custom-call(s32[8]{0:T(128)S(1)} %copy-done.3, s32[1]{0:T(128)} %bitcast.position_ref, bf16[512,384]{1,0:T(8,128)(2,1)S(1)} %collective-permute-done.prior_ref, bf16[3,3456,384]{2,1,0:T(8,128)(2,1)S(1)} %bitcast.15, f32[512,384]{1,0:T(8,128)S(1)} %local_conv.1.local_ref, ...), custom_call_target="tpu_custom_call" | custom-call | tf_op jit(solution)/shard_map/residual/pallas_call | solution.py:265
  50.3 3.0 %collective-permute-start.1 = (bf16[512,384]{1,0:T(8,128)(2,1)S(1)}, bf16[512,384]{1,0:T(8,128)(2,1)S(1)}, u32[]{:S(2)}, u32[]{:S(2)}) collective-permute-start(bf16[512,384]{1,0:T(8,128)(2,1)S(1)} %residual.1.residual_ref), channel_id=1, source_target_pairs={{0,1},{1,2},{2,3},{3,4},{4,5},{5,6},{6,7},{7,8},{8,9},{9,10},{10,1... | collective-permute-start | bytes 1179656 | tf_op jit(solution)/shard_map/ppermute | solution.py:38
  53.3 1.2 %fusion.2 = (bf16[2,2,1,384,192]{3,4,2,1,0:T(8,128)(2,1)}, bf16[2,2,1,384,192]{3,4,2,1,0:T(8,128)(2,1)}) fusion(f32[1,2,3,384,192]{3,4,2,1,0:T(8,128)S(1)} %copy-done.6, f32[1,2,3,384,192]{3,4,2,1,0:T(8,128)S(1)} %get-tuple-element.17), kind=kLoop, calls=%fused_computation.14 | loop fusion | flops 589824 | bytes 4718592 | tf_op jit(solution)/shard_map/convert.4
  54.6 1.3 %copy.13 = bf16[2,2,1,384,192]{4,3,1,0,2:T(8,128)(2,1)S(1)} copy(bf16[2,2,1,384,192]{3,4,2,1,0:T(8,128)(2,1)} %get-tuple-element.11) | data formatting | bytes 1179648 | tf_op jit(solution)/shard_map/convert.5
  55.9 0.0 copy-start.8
  55.9 0.3 copy.14
  56.2 1.3 %copy.15 = bf16[2,2,1,384,192]{4,3,1,0,2:T(8,128)(2,1)S(1)} copy(bf16[2,2,1,384,192]{3,4,2,1,0:T(8,128)(2,1)} %get-tuple-element.10) | data formatting | bytes 1179648 | tf_op jit(solution)/shard_map/convert.3
  57.5 2.2 %copy.12 = bf16[2,2,1,384,192]{4,3,1,0,2:T(8,128)(2,1)} copy(bf16[2,2,1,384,192]{3,4,2,1,0:T(8,128)(2,1)} %get-tuple-element.9) | data formatting | bytes 1179648 | tf_op jit(solution)/shard_map/convert.4
  59.8 1.9 %maximum_maximum_fusion.folded_ref = bf16[2,2,2,768,192]{4,3,2,1,0:T(8,128)(2,1)S(1)} fusion(bf16[1,1,2,768,192]{4,3,2,1,0:T(8,128)(2,1)S(1)} %bitcast.21, bf16[1,1,2,768,192]{4,3,2,1,0:T(8,128)(2,1)S(1)} %bitcast.20, bf16[1,1,2,768,192]{4,3,2,1,0:T(8,128)(2,1)S(1)} %bitcast.19, bf16[1,1,2,768,192]{4,3,2,1,0:T(8,128)(2,1)} %bitcast.22), kind=kLoop, calls=%fused_computation.4 | loop fusion | flops 3538944 | bytes 4718592 | tf_op jit(solution)/shard_map/stack | solution.py:207
  61.7 0.0 copy-start.5
  61.7 1.3 %local_time.1.local_ref = f32[512,768]{1,0:T(8,128)S(1)} custom-call(s32[8]{0:T(128)S(1)} %copy-done.3, s32[1]{0:T(128)} %bitcast.position_ref, bf16[512,384]{1,0:T(8,128)(2,1)S(1)} %residual.1.residual_ref, bf16[3,384,768]{2,1,0:T(8,128)(2,1)S(1)} %copy-done.1, f32[1,768]{1,0:T(1,128)S(1)} %reshape.81.bias_ref), custom_call_target="tpu_custom_call" | custom-call | flops 452984832 | tf_op jit(solution)/shard_map/local_time/pallas_call | solution.py:284
  63.0 7.0 %upscale.1 = bf16[4,32,6144]{2,1,0:T(8,128)(2,1)} custom-call(s32[8]{0:T(128)S(1)} %copy-done.3, s32[1]{0:T(128)} %bitcast.position_ref, bf16[512,384]{1,0:T(8,128)(2,1)S(1)} %collective-permute-done.1.prior_ref, bf16[3,384,768]{2,1,0:T(8,128)(2,1)S(1)} %copy-done.1, f32[512,768]{1,0:T(8,128)S(1)} %local_time.1.local_ref, ...), custom_call_target="tpu_custom_call" | custom-call | tf_op jit(solution)/shard_map/upscale/pallas_call | solution.py:296
  (19 shorter events, 0.0 us)
Async XLA Ops:
  0.0 1.0 %copy-start.2 = (bf16[512,384]{1,0:T(8,128)(2,1)S(1)}, bf16[512,384]{1,0:T(8,128)(2,1)}, u32[]{:S(2)}) copy-start(bf16[512,384]{1,0:T(8,128)(2,1)} %latent_ref.1) | copy-start | bytes 1179652
  1.0 0.7 copy-start.4
  1.7 9.4 %copy-start.7 = (bf16[3,3,384,192]{2,3,1,0:T(8,128)(2,1)S(1)}, bf16[3,3,384,192]{2,3,1,0:T(8,128)(2,1)}, u32[]{:S(2)}) copy-start(bf16[3,3,384,192]{2,3,1,0:T(8,128)(2,1)} %param.20) | copy-start | bytes 3981316
  3.7 26.1 %all-to-all-start = ((bf16[16,64,384]{2,1,0:T(8,128)(2,1)}), bf16[16,64,384]{2,1,0:T(8,128)(2,1)S(1)}, u32[]{:S(2)}, u32[]{:S(2)}) async-start(bf16[16,64,384]{2,1,0:T(8,128)(2,1)} %bitcast.2), calls=%async_computation | async-start | bytes 1572864 | tf_op jit(solution)/shard_map/all_to_all | solution.py:242
  11.1 0.7 copy-start.9
  11.1 0.7 copy-start.10
  31.2 15.4 %collective-permute-start = (bf16[512,384]{1,0:T(8,128)(2,1)S(1)}, bf16[512,384]{1,0:T(8,128)(2,1)S(1)}, u32[]{:S(2)}, u32[]{:S(2)}) collective-permute-start(bf16[512,384]{1,0:T(8,128)(2,1)S(1)} %get-tuple-element.7.active_ref), channel_id=1, source_target_pairs={{0,1},{1,2},{2,3},{3,4},{4,5},{5,6},{6,7},{7,8},{8,9},{9,10},{10,1... | collective-permute-start | bytes 1179656 | tf_op jit(solution)/shard_map/ppermute | solution.py:38
  33.4 3.5 %copy-start.11 = (f32[384]{0:T(512)S(1)}, f32[384]{0:T(512)}, u32[]{:S(2)}) copy-start(f32[384]{0:T(512)} %param.17) | copy-start | bytes 4612
  36.9 2.8 %copy-start.3 = (s32[8]{0:T(128)S(1)}, s32[8]{0:T(128)}, u32[]{:S(2)}) copy-start(s32[8]{0:T(128)} %counts_ref.7) | copy-start | bytes 100
  39.6 3.3 %copy-start = (bf16[3,3,3,384,384]{4,3,2,1,0:T(8,128)(2,1)S(1)}, bf16[3,3,3,384,384]{4,3,2,1,0:T(8,128)(2,1)}, u32[]{:S(2)}) copy-start(bf16[3,3,3,384,384]{4,3,2,1,0:T(8,128)(2,1)} %param.16) | copy-start | bytes 23887876
  46.6 6.7 %copy-start.6 = (f32[1,2,3,384,192]{3,4,2,1,0:T(8,128)S(1)}, f32[1,2,3,384,192]{3,4,2,1,0:T(8,128)}, u32[]{:S(2)}) copy-start(f32[1,2,3,384,192]{3,4,2,1,0:T(8,128)} %get-tuple-element.18) | copy-start | bytes 5308420
  50.3 12.7 %collective-permute-start.1 = (bf16[512,384]{1,0:T(8,128)(2,1)S(1)}, bf16[512,384]{1,0:T(8,128)(2,1)S(1)}, u32[]{:S(2)}, u32[]{:S(2)}) collective-permute-start(bf16[512,384]{1,0:T(8,128)(2,1)S(1)} %residual.1.residual_ref), channel_id=1, source_target_pairs={{0,1},{1,2},{2,3},{3,4},{4,5},{5,6},{6,7},{7,8},{8,9},{9,10},{10,1... | collective-permute-start | bytes 1179656 | tf_op jit(solution)/shard_map/ppermute | solution.py:38
  55.9 3.9 %copy-start.8 = (f32[768]{0:T(1024)S(1)}, f32[768]{0:T(1024)}, u32[]{:S(2)}) copy-start(f32[768]{0:T(1024)} %param.19) | copy-start | bytes 9220
  59.8 1.9 %copy-start.1 = (bf16[3,384,768]{2,1,0:T(8,128)(2,1)S(1)}, bf16[3,384,768]{2,1,0:T(8,128)(2,1)}, u32[]{:S(2)}) copy-start(bf16[3,384,768]{2,1,0:T(8,128)(2,1)} %kernel_ref.3) | copy-start | bytes 5308420
  61.7 1.3 %copy-start.5 = (f32[192]{0:T(256)S(1)}, f32[192]{0:T(256)}, u32[]{:S(2)}) copy-start(f32[192]{0:T(256)} %param.21) | copy-start | bytes 2308
where the time goes:
time: 71 us; the launch traced here: 70 us
  Pallas kernels  19 us (27%)
  waiting for transfers between devices  15.3 us (22%)
  starting transfers between devices  12.6 us (18%)
  local copies, waits for them, and re-layouts  12 us (17%)
  other arithmetic  10.9 us (15%)
    all_to_all x1, waiting for transfers between devices, on_device(): lax.all_to_all(packed, 'tm', split_axis=0, concat_axis=0, tiled=True)  15.3 us
    all_to_all x1, starting transfers between devices, on_device(): lax.all_to_all(packed, 'tm', split_axis=0, concat_axis=0, tiled=True)  7.39 us
    pallas_call x1, Pallas kernels, on_device(): pl.pallas_call(up_kernel_body, out_shape=jax.ShapeDtypeStruct((frames, 2...  6.98 us
    unnamed x24, local copies, waits for them, and re-layouts  5.44 us
    ppermute x2, starting transfers between devices, from_behind(): return lax.ppermute(value, axis, pairs)  5.24 us
    another operation x4, local copies, waits for them, and re-layouts  5.17 us
    another operation x2, other arithmetic  3.99 us
    pallas_call x1, Pallas kernels, on_device(): pl.pallas_call(residual_kernel, out_shape=pltpu.VMEM((tokens, channels),...  3.66 us
  transfers between devices with their start and end apart: 3, of which 1 were waited for; matrix products, arithmetic and copies ran while one was open for 25% of the time, Pallas kernels for 7%

commit v1 on v0

v1 whole, which is shorter than its diff:
```python
import functools

import jax
import jax.numpy as jnp
from jax import lax
from jax.experimental import pallas as pl
from jax.experimental.pallas import tpu as pltpu
from jax.sharding import PartitionSpec as P

H = 16
W = 16
MARK = 128.0
epsilon = 1e-06
MIB = 1 << 20
f32 = jnp.float32
bf16 = jnp.bfloat16


def in_vmem(value):
    return pltpu.with_memory_space_constraint(value, pltpu.VMEM)


def in_hbm(value):
    return pltpu.with_memory_space_constraint(value, pltpu.HBM)


VM = pl.BlockSpec(memory_space=pltpu.VMEM)
HB = pl.BlockSpec(memory_space=pltpu.HBM)
SM = pl.BlockSpec(memory_space=pltpu.SMEM)


def iota(shape, dim):
    return lax.broadcasted_iota(jnp.int32, shape, dim)


def mm(lhs, rhs):
    return jnp.dot(lhs, rhs, preferred_element_type=f32)


def from_behind(value, axis):
    size = lax.axis_size(axis)
    return lax.ppermute(value, axis, [(i, (i + 1) % size) for i in range(size)])


def pack_kernel(
    owner_hbm, latent_hbm, out_hbm, owner_ref, wide_ref, made_ref, arrived, left, *, peers, capacity
):
    tokens, channels = latent_hbm.shape
    copies = [
        pltpu.make_async_copy(owner_hbm, owner_ref, arrived.at[0]),
        pltpu.make_async_copy(latent_hbm, wide_ref.at[:, :channels], arrived.at[1]),
    ]
    for copy in copies:
        copy.start()
    wide_ref[:, channels:] = jnp.ones((tokens, 128), bf16)
    upper = (iota((tokens, tokens), 0) <= iota((tokens, tokens), 1)).astype(bf16)
    copies[0].wait()
    owner = owner_ref[...]
    marked = iota((peers, tokens), 0) == owner
    running = mm(marked.astype(bf16), upper)
    rank = jnp.sum(jnp.where(marked, running - 1.0, 0.0), 0, keepdims=True)
    slot = owner * capacity + rank.astype(jnp.int32)
    copies[1].wait()
    pieces = left.shape[0]
    rows = peers * capacity // pieces
    sent = []
    for piece in range(pieces):
        at = pl.ds(piece * rows, rows)
        chosen = (iota((rows, tokens), 0) + piece * rows == slot).astype(bf16)
        found = mm(chosen, wide_ref[...])
        empty = (1.0 - found[:, channels:]) * MARK
        made_ref[at] = (
            found[:, :channels] + jnp.concatenate([empty] * (channels // 128), 1)
        ).astype(bf16)
        copy = pltpu.make_async_copy(made_ref.at[at], out_hbm.at[at], left.at[piece])
        copy.start()
        sent.append(copy)
    for copy in sent:
        copy.wait()


def unpack_kernel(
    got_ref, small_ref, taps_hbm, decoded_ref, active_ref, taps_ref, arrived,
    *, peers, capacity, frame,
):
    copy = pltpu.make_async_copy(
        taps_hbm.at[1, pl.ds(frame * taps_ref.shape[0], taps_ref.shape[0])], taps_ref, arrived
    )
    copy.start()
    slots, channels = got_ref.shape
    pixels = decoded_ref.shape[0]
    present = (got_ref[:, :128] < MARK / 2).astype(bf16)
    slot_of = iota((peers, slots), 1)
    member = (slot_of // capacity == iota((peers, slots), 0)).astype(bf16)
    counts = mm(member, present)
    below = (iota((peers, peers), 1) < iota((peers, peers), 0)).astype(f32)
    before = jnp.dot(below, counts, precision=lax.Precision.HIGHEST, preferred_element_type=f32)
    member32 = member.astype(f32)
    first = jnp.sum(member32 * before[:, :1], 0, keepdims=True).astype(jnp.int32)
    held = jnp.sum(member32 * counts[:, :1], 0, keepdims=True).astype(jnp.int32)
    within = iota((1, slots), 1) % capacity
    place = jnp.where(within < held, first + within, -1)
    pixel = iota((pixels, slots), 0)
    source = frame * pixels + (pixel % H) * W + pixel // H
    chosen = (source == place).astype(bf16)
    values = mm(chosen, got_ref[...])
    decoded_ref[...] = values.astype(bf16)
    squares = jnp.mean(values * values, -1, keepdims=True)
    scaled = values * lax.rsqrt(squares + epsilon)
    fed = scaled * small_ref[0:1, :channels] + small_ref[1:2, :channels]
    active_ref[...] = (fed / (1.0 + jnp.exp(-fed))).astype(bf16)
    copy.wait()


def vertical(frame):
    wide = frame.astype(f32)
    y = iota(wide.shape, 0) % H
    up = jnp.where(y == 0, 0.0, pltpu.roll(wide, 1, 0))
    down = jnp.where(y == H - 1, 0.0, pltpu.roll(wide, wide.shape[0] - 1, 0))
    return up.astype(bf16), frame, down.astype(bf16)


def patches(frame):
    pixels, channels = frame.shape
    nothing = jnp.zeros((H, channels), bf16)
    parts = []
    for shifted in vertical(frame):
        parts.append(jnp.concatenate([nothing, shifted[: pixels - H]], 0))
        parts.append(shifted)
        parts.append(jnp.concatenate([shifted[H:], nothing], 0))
    return jnp.concatenate(parts, 1)


def kept(keep_ref):
    return [[keep_ref[3 * f + back : 3 * f + back + 1, :1] for back in range(3)] for f in range(2)]


def halved(near, low_ref, high_ref):
    half = low_ref.shape[0]
    return mm(near[:, :half], low_ref[...]) + mm(near[:, half:], high_ref[...])


def local_conv_kernel(
    keep_ref, first_ref, second_ref, low_ref, high_ref, here_ref, taps_hbm, time_hbm,
    sum0_ref, sum1_ref, taps_ref, time_ref,
    near, arrived,
):
    copies = [
        pltpu.make_async_copy(taps_hbm.at[0], taps_ref, arrived.at[0]),
        pltpu.make_async_copy(time_hbm, time_ref, arrived.at[1]),
    ]
    for copy in copies:
        copy.start()
    pixels = H * W
    keep = kept(keep_ref)
    near[:pixels] = patches(first_ref[...])
    near[pixels:] = patches(second_ref[...])
    own = mm(near[...], here_ref[...])
    sum0_ref[...] = own[:pixels]
    sum1_ref[...] = own[pixels:] + keep[1][1] * halved(near[:pixels], low_ref, high_ref)
    for copy in copies:
        copy.wait()


def second_residual_kernel(
    keep_ref, small_ref, prior_ref, taps_ref, sum_ref, decoded_ref, folded_hbm,
    out_ref, near_ref, folded_ref,
    arrived,
):
    copy = pltpu.make_async_copy(folded_hbm.at[0], folded_ref, arrived)
    copy.start()
    keep = kept(keep_ref)
    near_ref[...] = patches(prior_ref[...])
    base = sum_ref[...] + decoded_ref[...].astype(f32) + small_ref[2:3, : out_ref.shape[1]]
    out_ref[...] = (base + keep[1][2] * mm(near_ref[...], taps_ref[...])).astype(bf16)
    copy.wait()


def behind_kernel(
    keep_ref, small_ref, near_ref, low_ref, high_ref, sum_ref, decoded_ref, folded_hbm,
    out_ref, folded_ref,
    arrived,
):
    copy = pltpu.make_async_copy(folded_hbm.at[1], folded_ref, arrived)
    copy.start()
    keep = kept(keep_ref)
    base = sum_ref[...] + decoded_ref[...].astype(f32) + small_ref[2:3, : out_ref.shape[1]]
    out_ref[...] = base + keep[0][1] * halved(near_ref[...], low_ref, high_ref)
    copy.wait()


def first_residual_kernel(keep_ref, prior_ref, taps_ref, sum_ref, out_ref, near):
    keep = kept(keep_ref)
    near[...] = patches(prior_ref[...])
    out_ref[...] = (sum_ref[...] + keep[0][2] * mm(near[...], taps_ref[...])).astype(bf16)


def local_time_kernel(
    keep_ref, small_ref, first_ref, second_ref, time_ref, sum0_ref, sum1_ref
):
    keep = kept(keep_ref)
    bias = small_ref[3:4, : sum0_ref.shape[1]]
    sum0_ref[...] = mm(first_ref[...], time_ref[2]) + bias
    sum1_ref[...] = (
        mm(second_ref[...], time_ref[2]) + bias + keep[1][1] * mm(first_ref[...], time_ref[1])
    )


def upscale(temporal, frame, small_ref, even_ref, odd_ref, out_hbm, near, rows32, made, left):
    pixels = H * W
    channels = near.shape[1] // 3
    outs = even_ref.shape[3]
    both = temporal.astype(bf16)
    nothing = jnp.zeros((H, 3 * channels), bf16)
    for half in range(2):
        base = H + half * (pixels + H)
        near[base - H : base] = nothing
        shown = both[:, half * channels : (half + 1) * channels]
        for a, shifted in enumerate(vertical(shown)):
            near[base : base + pixels, a * channels : (a + 1) * channels] = shifted
    near[2 * (H + pixels) :] = nothing
    span = 2 * pixels + H
    bias = small_ref[4:5, :outs]
    blocks = 2 * outs // 128
    for p in range(2):
        phases = []
        for q, taps_ref in enumerate((even_ref, odd_ref)):
            total = bias
            for side in range(2):
                first = (q + side) * H
                window = near[first : first + span, p * channels : (p + 2) * channels]
                total = total + mm(window, taps_ref[side, p])
            phases.append(total)
        pair = jnp.concatenate(phases, 1)
        for half in range(2):
            for x in range(W):
                row = half * (pixels + H) + x * H
                for block in range(blocks):
                    rows32[half, x * blocks + block, pl.ds(p, H, stride=2)] = pair[
                        row : row + H, block * 128 : (block + 1) * 128
                    ]
    sent = []
    for half in range(2):
        for block in range(W * blocks):
            made[half, :, block * 128 : (block + 1) * 128] = rows32[half, block].astype(bf16)
        copy = pltpu.make_async_copy(made.at[half], out_hbm.at[2 * frame + half], left.at[half])
        copy.start()
        sent.append(copy)
    for copy in sent:
        copy.wait()


def second_up_kernel(
    keep_ref, small_ref, prior_ref, time_ref, sum_ref, even_ref, odd_ref, out_hbm,
    near, rows32, made, left,
):
    keep = kept(keep_ref)
    temporal = sum_ref[...] + keep[1][2] * mm(prior_ref[...], time_ref[0])
    upscale(temporal, 1, small_ref, even_ref, odd_ref, out_hbm, near, rows32, made, left)


def first_up_kernel(
    keep_ref, small_ref, before_ref, prior_ref, time_ref, sum_ref, even_ref, odd_ref, made_hbm,
    out_hbm,
    near, rows32, made, left,
):
    keep = kept(keep_ref)
    far = keep[0][2] * mm(before_ref[...], time_ref[0])
    temporal = sum_ref[...] + far + keep[0][1] * mm(prior_ref[...], time_ref[1])
    upscale(temporal, 0, small_ref, even_ref, odd_ref, out_hbm, near, rows32, made, left)


def keeps(counts_ref, position_ref):
    first = position_ref[0] * 2
    starts = [jnp.int32(0), jnp.int32(0)]
    end = jnp.int32(0)
    for video in range(counts_ref.shape[0]):
        end = end + counts_ref[video]
        starts = [jnp.where(end <= first + f, end, starts[f]) for f in range(2)]
    return [
        [(first + f - back >= starts[f]).astype(f32) for back in range(3)] for f in range(2)
    ]


def halves(taps):
    return (taps[0], taps[1] + taps[2]), (taps[0] + taps[1], taps[2])


def prepare_kernel(
    counts_ref, position_ref, gain_ref, shift_ref, res_bias_ref, time_bias_ref, up_bias_ref,
    up_hbm, taps_hbm,
    folded_ref, small_ref, keep_ref, taps_ref,
    up_ref, arrived,
):
    copies = [
        pltpu.make_async_copy(up_hbm, up_ref, arrived.at[0]),
        pltpu.make_async_copy(taps_hbm.at[2], taps_ref, arrived.at[1]),
    ]
    for copy in copies:
        copy.start()
    small_ref[...] = jnp.zeros_like(small_ref)
    for i, ref in enumerate((gain_ref, shift_ref, res_bias_ref, time_bias_ref, up_bias_ref)):
        small_ref[i : i + 1, : ref.shape[1]] = ref[...]
    keep = keeps(counts_ref, position_ref)
    row = iota(keep_ref.shape, 0)
    seen = jnp.zeros(keep_ref.shape, f32)
    for f in range(2):
        for back in range(3):
            seen = jnp.where(row == 3 * f + back, keep[f][back], seen)
    keep_ref[...] = seen
    copies[0].wait()
    channels = up_ref.shape[3]
    columns = [
        halves([up_ref[a, b].astype(f32) for b in range(3)]) for a in range(3)
    ]
    for q in range(2):
        for side in range(2):
            rows = halves([columns[a][q][side] for a in range(3)])
            for p in range(2):
                for dy in range(2):
                    folded_ref[q, side, p, dy * channels : (dy + 1) * channels] = rows[p][
                        dy
                    ].T.astype(bf16)
    copies[1].wait()


def on_device(
    latent,
    owner,
    frame_counts,
    norm_gain,
    norm_shift,
    res_kernel,
    res_bias,
    time_kernel,
    time_bias,
    up_kernel,
    up_bias,
):
    peers = lax.axis_size("tm")
    position = lax.axis_index("tm").astype(jnp.int32).reshape(1)
    tokens, channels = latent.shape
    capacity = 2 * tokens // peers
    pixels = H * W
    wide = time_kernel.shape[-1]
    outs = up_kernel.shape[-1]

    packed = pl.pallas_call(
        functools.partial(pack_kernel, peers=peers, capacity=capacity),
        out_shape=jax.ShapeDtypeStruct((peers * capacity, channels), bf16),
        in_specs=[HB, HB],
        out_specs=HB,
        scratch_shapes=[
            pltpu.VMEM((1, tokens), jnp.int32),
            pltpu.VMEM((tokens, channels + 128), bf16),
            pltpu.VMEM((peers * capacity, channels), bf16),
            pltpu.SemaphoreType.DMA((2,)),
            pltpu.SemaphoreType.DMA((4,)),
        ],
        compiler_params=pltpu.CompilerParams(vmem_limit_bytes=16 * MIB),
        name="pack",
    )(in_hbm(owner.reshape(1, tokens)), in_hbm(latent))
    packed, up_kernel = lax.optimization_barrier((packed, up_kernel))
    received = lax.all_to_all(packed, "tm", split_axis=0, concat_axis=0, tiled=True)
    res_kernel = in_hbm(res_kernel.reshape(3, 9 * channels, channels))
    folded, small, keep, here = pl.pallas_call(
        prepare_kernel,
        out_shape=[
            jax.ShapeDtypeStruct((2, 2, 2, 2 * channels, outs), bf16),
            pltpu.VMEM((8, wide), f32),
            pltpu.VMEM((8, 128), f32),
            pltpu.VMEM((9 * channels, channels), bf16),
        ],
        in_specs=[SM] * 2 + [VM] * 5 + [HB] * 2,
        out_specs=[VM] * 4,
        scratch_shapes=[
            pltpu.VMEM((3, 3, outs, channels), bf16),
            pltpu.SemaphoreType.DMA((2,)),
        ],
        compiler_params=pltpu.CompilerParams(vmem_limit_bytes=16 * MIB),
        cost_estimate=pl.CostEstimate(
            flops=0, bytes_accessed=2 * res_kernel.size * 2, transcendentals=0
        ),
        name="prepare",
    )(
        frame_counts,
        position,
        norm_gain.reshape(1, channels),
        norm_shift.reshape(1, channels),
        res_bias.reshape(1, channels),
        time_bias.reshape(1, wide),
        up_bias.reshape(1, outs),
        in_hbm(jnp.swapaxes(up_kernel, 2, 3)),
        res_kernel,
    )

    def call(body, name, outputs, arguments, scratch=(), flops=0, **more):
        out_specs = more.pop("out_specs", [VM] * len(outputs))
        in_specs = more.pop("in_specs", [VM] * len(arguments))
        return pl.pallas_call(
            body,
            out_shape=outputs,
            in_specs=in_specs,
            out_specs=out_specs,
            scratch_shapes=scratch,
            compiler_params=pltpu.CompilerParams(vmem_limit_bytes=12 * MIB),
            cost_estimate=pl.CostEstimate(flops=flops, bytes_accessed=0, transcendentals=0),
            name=name,
            **more,
        )(*arguments)

    vm = in_vmem
    frame16 = pltpu.VMEM((pixels, channels), bf16)
    frame32 = pltpu.VMEM((pixels, channels), f32)
    near_shape = pltpu.VMEM((pixels, 9 * channels), bf16)
    tap = 2 * pixels * 9 * channels * channels
    sem = pltpu.SemaphoreType.DMA
    taps_shape = pltpu.VMEM((9 * channels, channels), bf16)
    small, keep, received = vm(small), vm(keep), vm(received)
    decoded, active, prior, behind = {}, {}, {}, {}
    for f in (1, 0):
        decoded[f], active[f], behind[f] = call(
            functools.partial(unpack_kernel, peers=peers, capacity=capacity, frame=f),
            "unpack",
            [frame16] * 2 + [pltpu.VMEM((9 * channels // 2, channels), bf16)],
            [received, small, res_kernel],
            [sem],
            in_specs=[VM, VM, HB],
        )
        prior[f] = from_behind(active[f], "tm")
    low, high, here = vm(behind[0]), vm(behind[1]), vm(here)
    sum0, sum1, far, times = call(
        local_conv_kernel,
        "local_conv",
        [frame32] * 2 + [taps_shape, pltpu.VMEM(time_kernel.shape, bf16)],
        [keep, vm(active[0]), vm(active[1]), low, high, here, res_kernel, in_hbm(time_kernel)],
        [pltpu.VMEM((2 * pixels, 9 * channels), bf16), sem((2,))],
        flops=3 * tap,
        in_specs=[VM] * 6 + [HB] * 2,
    )
    far, folded = vm(far), in_hbm(folded)
    half_taps = pltpu.VMEM(folded.shape[1:], bf16)
    second, near, taps0 = call(
        second_residual_kernel,
        "second_residual",
        [frame16, near_shape, half_taps],
        [keep, small, vm(prior[1]), far, vm(sum1), vm(decoded[1]), folded],
        [sem],
        flops=tap,
        in_specs=[VM] * 6 + [HB],
    )
    prior_second = from_behind(second, "tm")
    sum0, taps1 = call(
        behind_kernel,
        "behind",
        [frame32, half_taps],
        [keep, small, vm(near), low, high, vm(sum0), vm(decoded[0]), folded],
        [sem],
        flops=tap,
        in_specs=[VM] * 7 + [HB],
    )
    (first,) = call(
        first_residual_kernel,
        "first_residual",
        [frame16],
        [keep, vm(prior[0]), far, vm(sum0)],
        [near_shape],
        flops=tap,
    )
    prior_first = from_behind(first, "tm")
    times = vm(times)
    time0, time1 = call(
        local_time_kernel,
        "local_time",
        [pltpu.VMEM((pixels, wide), f32)] * 2,
        [keep, small, vm(first), vm(second), times],
        flops=6 * pixels * channels * wide,
    )
    frames = 2 * tokens // pixels
    out = jax.ShapeDtypeStruct((frames, 2 * H, 2 * W * outs), bf16)
    up_scratch = [
        pltpu.VMEM((2 * pixels + 3 * H, 3 * channels), bf16),
        pltpu.VMEM((2, 2 * W * outs // 128, 2 * H, 128), f32),
        pltpu.VMEM((2, 2 * H, 2 * W * outs), bf16),
        sem((2,)),
    ]
    taps0, taps1, prior_second = vm(taps0), vm(taps1), vm(prior_second)
    (made,) = call(
        second_up_kernel,
        "second_up",
        [out],
        [keep, small, prior_second, times, vm(time1), taps0, taps1],
        up_scratch,
        flops=8 * tap,
        out_specs=[HB],
    )
    (made,) = call(
        first_up_kernel,
        "first_up",
        [out],
        [keep, small, vm(prior_first), prior_second, times, vm(time0), taps0, taps1, made],
        up_scratch,
        flops=8 * tap,
        in_specs=[VM] * 8 + [pl.BlockSpec(memory_space=pl.ANY)],
        out_specs=[HB],
        input_output_aliases={8: 0},
    )
    return made


def solution(mesh):
    placed = (
        P(("groups", "tm"), None),
        P(("groups", "tm")),
        P("groups"),
        P(),
        P(),
        P(),
        P(),
        P(),
        P(),
        P(),
        P(),
    )
    return jax.shard_map(
        on_device,
        mesh=mesh,
        in_specs=placed,
        out_specs=P(("groups", "tm"), None, None),
        check_vma=False,
    )
```

time: 71 us -> 54.4 us (0.77)
  other arithmetic: 10.9 us -> 0 us
  local copies, waits for them, and re-layouts: 12 us -> 1.67 us
  waiting for transfers between devices: 15.3 us -> 19.7 us
  Pallas kernels: 19 us -> 22.7 us
  starting transfers between devices: 12.6 us -> 9.6 us
    another operation x4 -> x0, other arithmetic: 9.32 us -> none
    ppermute x2 -> x4, waiting for transfers between devices: 0.01 us -> 5.63 us  [from_behind(): return lax.ppermute(value, axis, [(i, (i + 1) % size) for i in range(size)])]
    another operation x4 -> x0, local copies, waits for them, and re-layouts: 5.17 us -> none
    unnamed x24 -> x14, local copies, waits for them, and re-layouts: 5.44 us -> 1.66 us
    pallas_call x5 -> x10, Pallas kernels: 17 us -> 20.2 us  [the longest x9 17.3 us: call(): pl.pallas_call(body, out_shape=outputs, in_specs=in_specs, out_specs=out_...]
    ppermute x2 -> x4, starting transfers between devices: 5.24 us -> 2.2 us  [from_behind(): return lax.ppermute(value, axis, [(i, (i + 1) % size) for i in range(size)])]
    slice x1 -> x0, local copies, waits for them, and re-layouts: 1.35 us -> none  [fold(): taps[0]]
    add x1 -> x0, other arithmetic: 1.35 us -> none  [fold(): taps[1] + taps[2]]
  transfers between devices with their start and end apart: 3 -> 5, of which waited for: 1 -> 3; matrix products, arithmetic and copies ran while one was open for 25% -> 0% of each run, Pallas kernels for 7% -> 28%
where the time goes in v1:
time: 54.4 us; the launch traced here: 54.1 us
  Pallas kernels  22.7 us (42%)
  waiting for transfers between devices  19.7 us (36%)
  starting transfers between devices  9.6 us (18%)
  local copies, waits for them, and re-layouts  1.67 us (3%)
    pallas_call x9, Pallas kernels, call(): pl.pallas_call(body, out_shape=outputs, in_specs=in_specs, out_specs=out_...  17.3 us
    all_to_all x1, waiting for transfers between devices, on_device(): lax.all_to_all(packed, 'tm', split_axis=0, concat_axis=0, tiled=True)  14.1 us
    all_to_all x1, starting transfers between devices, on_device(): lax.all_to_all(packed, 'tm', split_axis=0, concat_axis=0, tiled=True)  7.4 us
    ppermute x4, waiting for transfers between devices, from_behind(): return lax.ppermute(value, axis, [(i, (i + 1) % size) for i in range(size)])  5.63 us
    pallas_call x1, Pallas kernels, on_device(): pl.pallas_call(prepare_kernel, out_shape=[jax.ShapeDtypeStruct((2, 2, 2,...  2.86 us
    pallas_call x1, Pallas kernels, on_device(): pl.pallas_call(functools.partial(pack_kernel, peers=peers, capacity=capac...  2.54 us
    ppermute x4, starting transfers between devices, from_behind(): return lax.ppermute(value, axis, [(i, (i + 1) % size) for i in range(size)])  2.2 us
    unnamed x14, local copies, waits for them, and re-layouts  1.66 us
  transfers between devices with their start and end apart: 5, of which 3 were waited for; matrix products, arithmetic and copies ran while one was open for 0% of the time, Pallas kernels for 28%

profile of v1, /device:TPU:0, one launch (start us, length us, event | category | flops | bytes accessed | tf_op | source)
XLA Modules:
  0.0 54.1 jit_solution(10396405510666731293)
XLA Ops:
  0.0 0.0 copy-start.5
  0.0 0.0 copy-start.6
  0.0 0.0 copy-start.2
  0.0 2.5 %pack.1 = bf16[1024,384]{1,0:T(8,128)(2,1)} custom-call(s32[1,512]{1,0:T(1,128)} %bitcast.15, bf16[512,384]{1,0:T(8,128)(2,1)} %latent_hbm.1), custom_call_target="tpu_custom_call" | custom-call | tf_op jit(solution)/shard_map/pack/pallas_call | solution.py:348
  2.6 7.4 %all-to-all-start = ((bf16[16,64,384]{2,1,0:T(8,128)(2,1)}), bf16[16,64,384]{2,1,0:T(8,128)(2,1)S(1)}, u32[]{:S(2)}, u32[]{:S(2)}) async-start(bf16[16,64,384]{2,1,0:T(8,128)(2,1)} %bitcast.5), calls=%async_computation | async-start | bytes 1572864 | tf_op jit(solution)/shard_map/all_to_all | solution.py:364
  10.0 0.0 copy-done.4
  10.0 0.0 copy-done.5
  10.0 0.0 copy-done.6
  10.0 0.0 copy-done.3
  10.1 0.0 copy-done.1
  10.1 0.0 copy-done.2
  10.1 2.9 %prepare.1 = (bf16[2,2,2,768,192]{4,3,2,1,0:T(8,128)(2,1)S(1)}, f32[8,768]{1,0:T(8,128)S(1)}, f32[8,128]{1,0:T(8,128)S(1)}, bf16[3456,384]{1,0:T(8,128)(2,1)S(1)}) custom-call(s32[8]{0:T(128)S(1)} %copy-done.2, s32[1]{0:T(128)} %bitcast.position_ref, f32[1,384]{1,0:T(1,128)S(1)} %reshape.27.gain_ref, f32[1,384]{1,0:T(1,128)S(1)} %reshape.28.shift_ref, ...), custom_call_target="tpu_custom_call" | custom-call | bytes 15925248 | tf_op jit(solution)/shard_map/prepare/pallas_call | solution.py:366
  13.0 0.0 copy-start
  13.0 1.6 %copy-done = bf16[2,2,2,768,192]{4,3,2,1,0:T(8,128)(2,1)} copy-done((bf16[2,2,2,768,192]{4,3,2,1,0:T(8,128)(2,1)}, bf16[2,2,2,768,192]{4,3,2,1,0:T(8,128)(2,1)S(1)}, u32[]{:S(2)}) %copy-start) | copy-done | bytes 2359320
  14.6 14.1 %all-to-all-done = bf16[16,64,384]{2,1,0:T(8,128)(2,1)S(1)} async-done(((bf16[16,64,384]{2,1,0:T(8,128)(2,1)}), bf16[16,64,384]{2,1,0:T(8,128)(2,1)S(1)}, u32[]{:S(2)}, u32[]{:S(2)}) %all-to-all-start) | async-done | bytes 786464 | tf_op jit(solution)/shard_map/all_to_all | solution.py:364
  28.7 1.4 %unpack.3 = (bf16[256,384]{1,0:T(8,128)(2,1)S(1)}, bf16[256,384]{1,0:T(8,128)(2,1)S(1)}, bf16[1728,384]{1,0:T(8,128)(2,1)S(1)}) custom-call(bf16[1024,384]{1,0:T(8,128)(2,1)S(1)} %bitcast.7, f32[8,768]{1,0:T(8,128)S(1)} %get-tuple-element.30.small_ref, bf16[3,3456,384]{2,1,0:T(8,128)(2,1)} %bitcast.11), custom_call_target="tpu_custom_call" | custom-call | tf_op jit(solution)/shard_map/unpack/pallas_call | solution.py:400
  30.1 0.3 collective-permute-start.1
  30.4 1.4 %unpack.2 = (bf16[256,384]{1,0:T(8,128)(2,1)S(1)}, bf16[256,384]{1,0:T(8,128)(2,1)S(1)}, bf16[1728,384]{1,0:T(8,128)(2,1)S(1)}) custom-call(bf16[1024,384]{1,0:T(8,128)(2,1)S(1)} %bitcast.8, f32[8,768]{1,0:T(8,128)S(1)} %get-tuple-element.30.small_ref, bf16[3,3456,384]{2,1,0:T(8,128)(2,1)} %bitcast.12), custom_call_target="tpu_custom_call" | custom-call | tf_op jit(solution)/shard_map/unpack/pallas_call | solution.py:400
  31.8 1.0 %collective-permute-start = (bf16[256,384]{1,0:T(8,128)(2,1)S(1)}, bf16[256,384]{1,0:T(8,128)(2,1)S(1)}, u32[]{:S(2)}, u32[]{:S(2)}) collective-permute-start(bf16[256,384]{1,0:T(8,128)(2,1)S(1)} %get-tuple-element.32.first_ref), channel_id=1, source_target_pairs={{0,1},{1,2},{2,3},{3,4},{4,5},{5,6},{6,7},{7,8},{8,9},{9,10},{10,1... | collective-permute-start | bytes 589832 | tf_op jit(solution)/shard_map/ppermute | solution.py:42
  32.8 3.1 %local_conv.1 = (f32[256,384]{1,0:T(8,128)S(1)}, f32[256,384]{1,0:T(8,128)S(1)}, bf16[3456,384]{1,0:T(8,128)(2,1)S(1)}, bf16[3,384,768]{2,1,0:T(8,128)(2,1)S(1)}) custom-call(f32[8,128]{1,0:T(8,128)S(1)} %get-tuple-element.29.keep_ref, bf16[256,384]{1,0:T(8,128)(2,1)S(1)} %get-tuple-element.32.first_ref, bf16[256,384]{1,0:T(8,128)(2,1)S(1)} %get-tuple-element.33.second_ref, ...), custom_call_target="tpu_custom_call" | custom-call | flops 2038431744 | tf_op jit(solution)/shard_map/local_conv/pallas_call | solution.py:400
  35.9 2.0 %collective-permute-done.1.prior_ref = bf16[256,384]{1,0:T(8,128)(2,1)S(1)} collective-permute-done((bf16[256,384]{1,0:T(8,128)(2,1)S(1)}, bf16[256,384]{1,0:T(8,128)(2,1)S(1)}, u32[]{:S(2)}, u32[]{:S(2)}) %collective-permute-start.1) | collective-permute-done | bytes 196640 | tf_op jit(solution)/shard_map/ppermute | solution.py:42
  37.9 1.4 %second_residual.1 = (bf16[256,384]{1,0:T(8,128)(2,1)S(1)}, bf16[256,3456]{1,0:T(8,128)(2,1)S(1)}, bf16[2,2,768,192]{3,2,1,0:T(8,128)(2,1)S(1)}) custom-call(f32[8,128]{1,0:T(8,128)S(1)} %get-tuple-element.29.keep_ref, f32[8,768]{1,0:T(8,128)S(1)} %get-tuple-element.30.small_ref, bf16[256,384]{1,0:T(8,128)(2,1)S(1)} %collective-permute-done.1.prior_ref, ...), custom_call_target="tpu_custom_call" | custom-call | flops 679477248 | tf_op jit(solution)/shard_map/second_residual/pallas_call | solution.py:400
  39.4 0.1 collective-permute-start.3
  39.5 1.4 %behind.1 = (f32[256,384]{1,0:T(8,128)S(1)}, bf16[2,2,768,192]{3,2,1,0:T(8,128)(2,1)S(1)}) custom-call(f32[8,128]{1,0:T(8,128)S(1)} %get-tuple-element.29.keep_ref, f32[8,768]{1,0:T(8,128)S(1)} %get-tuple-element.30.small_ref, bf16[256,3456]{1,0:T(8,128)(2,1)S(1)} %get-tuple-element.41.near_ref, bf16[1728,384]{1,0:T(8,128)(2,1)S(1)} %get-tuple-element.34.low_ref, ...), custom_call_target="tpu_custom_call" | custom-call | flops 679477248 | tf_op jit(solution)/shard_map/behind/pallas_call | solution.py:400
  40.9 0.0 collective-permute-done.prior_ref
  40.9 1.1 %first_residual.1.first_ref = bf16[256,384]{1,0:T(8,128)(2,1)S(1)} custom-call(f32[8,128]{1,0:T(8,128)S(1)} %get-tuple-element.29.keep_ref, bf16[256,384]{1,0:T(8,128)(2,1)S(1)} %collective-permute-done.prior_ref, bf16[3456,384]{1,0:T(8,128)(2,1)S(1)} %get-tuple-element.37.taps_ref, f32[256,384]{1,0:T(8,128)S(1)} %get-tuple-element.44.sum_ref), custom_call_target="tpu_custom_call" | custom-call | flops 679477248 | tf_op jit(solution)/shard_map/first_residual/pallas_call | solution.py:400
  42.0 0.8 %collective-permute-start.2 = (bf16[256,384]{1,0:T(8,128)(2,1)S(1)}, bf16[256,384]{1,0:T(8,128)(2,1)S(1)}, u32[]{:S(2)}, u32[]{:S(2)}) collective-permute-start(bf16[256,384]{1,0:T(8,128)(2,1)S(1)} %first_residual.1.first_ref), channel_id=1, source_target_pairs={{0,1},{1,2},{2,3},{3,4},{4,5},{5,6},{6,7},{7,8},{8,9},{9,10},{10,1... | collective-permute-start | bytes 589832 | tf_op jit(solution)/shard_map/ppermute | solution.py:42
  42.9 0.8 %local_time.1 = (f32[256,768]{1,0:T(8,128)S(1)}, f32[256,768]{1,0:T(8,128)S(1)}) custom-call(f32[8,128]{1,0:T(8,128)S(1)} %get-tuple-element.29.keep_ref, f32[8,768]{1,0:T(8,128)S(1)} %get-tuple-element.30.small_ref, bf16[256,384]{1,0:T(8,128)(2,1)S(1)} %first_residual.1.first_ref, bf16[256,384]{1,0:T(8,128)(2,1)S(1)} %get-tuple-element.45.second_ref, ...), custom_call_target="tpu_custom_call" | custom-call | flops 452984832 | tf_op jit(solution)/shard_map/local_time/pallas_call | solution.py:400
  43.7 3.6 %collective-permute-done.3.prior_ref = bf16[256,384]{1,0:T(8,128)(2,1)S(1)} collective-permute-done((bf16[256,384]{1,0:T(8,128)(2,1)S(1)}, bf16[256,384]{1,0:T(8,128)(2,1)S(1)}, u32[]{:S(2)}, u32[]{:S(2)}) %collective-permute-start.3) | collective-permute-done | bytes 196640 | tf_op jit(solution)/shard_map/ppermute | solution.py:42
  47.2 3.2 %second_up.1.made_hbm = bf16[4,32,6144]{2,1,0:T(8,128)(2,1)} custom-call(f32[8,128]{1,0:T(8,128)S(1)} %get-tuple-element.29.keep_ref, f32[8,768]{1,0:T(8,128)S(1)} %get-tuple-element.30.small_ref, bf16[256,384]{1,0:T(8,128)(2,1)S(1)} %collective-permute-done.3.prior_ref, bf16[3,384,768]{2,1,0:T(8,128)(2,1)S(1)} %get-tuple-element.46.time_ref, ...), custom_call_target="tpu_custom_call" | custom-call | flops 5435817984 | tf_op jit(solution)/shard_map/second_up/pallas_call | solution.py:400
  50.5 0.0 collective-permute-done.2.before_ref
  50.5 3.5 %first_up.1 = bf16[4,32,6144]{2,1,0:T(8,128)(2,1)} custom-call(f32[8,128]{1,0:T(8,128)S(1)} %get-tuple-element.29.keep_ref, f32[8,768]{1,0:T(8,128)S(1)} %get-tuple-element.30.small_ref, bf16[256,384]{1,0:T(8,128)(2,1)S(1)} %collective-permute-done.2.before_ref, ...), custom_call_target="tpu_custom_call", output_to_operand_aliasing={{}: (8, {})} | custom-call | flops 5435817984 | tf_op jit(solution)/shard_map/first_up/pallas_call | solution.py:400
  (7 shorter events, 0.0 us)
Async XLA Ops:
  0.0 10.0 %copy-start.4 = (f32[384]{0:T(512)S(1)}, f32[384]{0:T(512)}, u32[]{:S(2)}) copy-start(f32[384]{0:T(512)} %param.14) | copy-start | bytes 4612
  0.0 10.0 %copy-start.5 = (f32[384]{0:T(512)S(1)}, f32[384]{0:T(512)}, u32[]{:S(2)}) copy-start(f32[384]{0:T(512)} %param.15) | copy-start | bytes 4612
  0.0 10.0 %copy-start.6 = (f32[384]{0:T(512)S(1)}, f32[384]{0:T(512)}, u32[]{:S(2)}) copy-start(f32[384]{0:T(512)} %param.17) | copy-start | bytes 4612
  0.0 10.0 %copy-start.3 = (f32[768]{0:T(1024)S(1)}, f32[768]{0:T(1024)}, u32[]{:S(2)}) copy-start(f32[768]{0:T(1024)} %param.19) | copy-start | bytes 9220
  0.0 10.1 %copy-start.1 = (f32[192]{0:T(256)S(1)}, f32[192]{0:T(256)}, u32[]{:S(2)}) copy-start(f32[192]{0:T(256)} %param.21) | copy-start | bytes 2308
  0.0 10.1 %copy-start.2 = (s32[8]{0:T(128)S(1)}, s32[8]{0:T(128)}, u32[]{:S(2)}) copy-start(s32[8]{0:T(128)} %counts_ref.1) | copy-start | bytes 100
  2.6 26.1 %all-to-all-start = ((bf16[16,64,384]{2,1,0:T(8,128)(2,1)}), bf16[16,64,384]{2,1,0:T(8,128)(2,1)S(1)}, u32[]{:S(2)}, u32[]{:S(2)}) async-start(bf16[16,64,384]{2,1,0:T(8,128)(2,1)} %bitcast.5), calls=%async_computation | async-start | bytes 1572864 | tf_op jit(solution)/shard_map/all_to_all | solution.py:364
  13.0 1.6 %copy-start = (bf16[2,2,2,768,192]{4,3,2,1,0:T(8,128)(2,1)}, bf16[2,2,2,768,192]{4,3,2,1,0:T(8,128)(2,1)S(1)}, u32[]{:S(2)}) copy-start(bf16[2,2,2,768,192]{4,3,2,1,0:T(8,128)(2,1)S(1)} %get-tuple-element.40.folded_hbm) | copy-start | bytes 7077892
  30.1 7.8 %collective-permute-start.1 = (bf16[256,384]{1,0:T(8,128)(2,1)S(1)}, bf16[256,384]{1,0:T(8,128)(2,1)S(1)}, u32[]{:S(2)}, u32[]{:S(2)}) collective-permute-start(bf16[256,384]{1,0:T(8,128)(2,1)S(1)} %get-tuple-element.33.second_ref), channel_id=1, source_target_pairs={{0,1},{1,2},{2,3},{3,4},{4,5},{5,6},{6,7},{7,8},{8,9},{9,10},{10,1... | collective-permute-start | bytes 589832 | tf_op jit(solution)/shard_map/ppermute | solution.py:42
  31.8 9.1 %collective-permute-start = (bf16[256,384]{1,0:T(8,128)(2,1)S(1)}, bf16[256,384]{1,0:T(8,128)(2,1)S(1)}, u32[]{:S(2)}, u32[]{:S(2)}) collective-permute-start(bf16[256,384]{1,0:T(8,128)(2,1)S(1)} %get-tuple-element.32.first_ref), channel_id=1, source_target_pairs={{0,1},{1,2},{2,3},{3,4},{4,5},{5,6},{6,7},{7,8},{8,9},{9,10},{10,1... | collective-permute-start | bytes 589832 | tf_op jit(solution)/shard_map/ppermute | solution.py:42
  39.4 7.8 %collective-permute-start.3 = (bf16[256,384]{1,0:T(8,128)(2,1)S(1)}, bf16[256,384]{1,0:T(8,128)(2,1)S(1)}, u32[]{:S(2)}, u32[]{:S(2)}) collective-permute-start(bf16[256,384]{1,0:T(8,128)(2,1)S(1)} %get-tuple-element.45.second_ref), channel_id=1, source_target_pairs={{0,1},{1,2},{2,3},{3,4},{4,5},{5,6},{6,7},{7,8},{8,9},{9,10},{10,1... | collective-permute-start | bytes 589832 | tf_op jit(solution)/shard_map/ppermute | solution.py:42
  42.0 8.4 %collective-permute-start.2 = (bf16[256,384]{1,0:T(8,128)(2,1)S(1)}, bf16[256,384]{1,0:T(8,128)(2,1)S(1)}, u32[]{:S(2)}, u32[]{:S(2)}) collective-permute-start(bf16[256,384]{1,0:T(8,128)(2,1)S(1)} %first_residual.1.first_ref), channel_id=1, source_target_pairs={{0,1},{1,2},{2,3},{3,4},{4,5},{5,6},{6,7},{7,8},{8,9},{9,10},{10,1... | collective-permute-start | bytes 589832 | tf_op jit(solution)/shard_map/ppermute | solution.py:42

commit v2 on v1

v2 whole, which is shorter than its diff:
```python
import functools

import jax
import jax.numpy as jnp
from jax import lax
from jax.experimental import pallas as pl
from jax.experimental.pallas import tpu as pltpu
from jax.sharding import PartitionSpec as P

H = 16
W = 16
MARK = 128.0
epsilon = 1e-06
MIB = 1 << 20
f32 = jnp.float32
bf16 = jnp.bfloat16


def in_vmem(value):
    return pltpu.with_memory_space_constraint(value, pltpu.VMEM)


def in_hbm(value):
    return pltpu.with_memory_space_constraint(value, pltpu.HBM)


VM = pl.BlockSpec(memory_space=pltpu.VMEM)
HB = pl.BlockSpec(memory_space=pltpu.HBM)
SM = pl.BlockSpec(memory_space=pltpu.SMEM)


def iota(shape, dim):
    return lax.broadcasted_iota(jnp.int32, shape, dim)


def mm(lhs, rhs):
    return jnp.dot(lhs, rhs, preferred_element_type=f32)


def alone(keep_ref, f):
    row = 3 * f + 1 + f
    return jnp.max(keep_ref[row : row + 1]) == 0.0


def convolve(near, taps):
    return lax.dot_general(taps, near, (((0,), (1,)), ((), ())), preferred_element_type=f32).T


def from_behind(value, axis):
    size = lax.axis_size(axis)
    return lax.ppermute(value, axis, [(i, (i + 1) % size) for i in range(size)])


def pack_kernel(
    owner_hbm, latent_hbm, out_hbm, owner_ref, wide_ref, made_ref, arrived, left, *, peers, capacity
):
    tokens, channels = latent_hbm.shape
    copies = [
        pltpu.make_async_copy(owner_hbm, owner_ref, arrived.at[0]),
        pltpu.make_async_copy(latent_hbm, wide_ref.at[:, :channels], arrived.at[1]),
    ]
    for copy in copies:
        copy.start()
    wide_ref[:, channels:] = jnp.ones((tokens, 128), bf16)
    upper = (iota((tokens, tokens), 0) <= iota((tokens, tokens), 1)).astype(bf16)
    copies[0].wait()
    owner = owner_ref[...]
    marked = iota((peers, tokens), 0) == owner
    running = mm(marked.astype(bf16), upper)
    rank = jnp.sum(jnp.where(marked, running - 1.0, 0.0), 0, keepdims=True)
    slot = owner * capacity + rank.astype(jnp.int32)
    copies[1].wait()
    pieces = left.shape[0]
    rows = peers * capacity // pieces
    sent = []
    for piece in range(pieces):
        at = pl.ds(piece * rows, rows)
        chosen = (iota((rows, tokens), 0) + piece * rows == slot).astype(bf16)
        found = mm(chosen, wide_ref[...])
        empty = (1.0 - found[:, channels:]) * MARK
        made_ref[at] = (
            found[:, :channels] + jnp.concatenate([empty] * (channels // 128), 1)
        ).astype(bf16)
        copy = pltpu.make_async_copy(made_ref.at[at], out_hbm.at[at], left.at[piece])
        copy.start()
        sent.append(copy)
    for copy in sent:
        copy.wait()


def places(got_ref, peers, capacity):
    slots = got_ref.shape[0]
    present = (got_ref[:, :128] < MARK / 2).astype(bf16)
    sender = iota((peers, slots), 1) // capacity
    member = (sender == iota((peers, slots), 0)).astype(f32)
    below = (sender < iota((peers, slots), 0)).astype(f32)
    tallies = mm(jnp.concatenate([member, below], 0).astype(bf16), present)
    held = jnp.sum(member * tallies[:peers, :1], 0, keepdims=True).astype(jnp.int32)
    first = jnp.sum(member * tallies[peers:, :1], 0, keepdims=True).astype(jnp.int32)
    within = iota((1, slots), 1) % capacity
    return jnp.where(within < held, first + within, -1)


def unpack(place, got_ref, small_ref, decoded_ref, active_ref, frame):
    slots, channels = got_ref.shape
    pixels = decoded_ref.shape[0]
    pixel = iota((pixels, slots), 0)
    source = frame * pixels + (pixel % H) * W + pixel // H
    chosen = (source == place).astype(bf16)
    values = mm(chosen, got_ref[...])
    decoded_ref[...] = values.astype(bf16)
    squares = jnp.mean(values * values, -1, keepdims=True)
    scaled = values * lax.rsqrt(squares + epsilon)
    fed = scaled * small_ref[0:1, :channels] + small_ref[1:2, :channels]
    active_ref[...] = (fed / (1.0 + jnp.exp(-fed))).astype(bf16)


def unpack_second_kernel(
    got_ref, small_ref, decoded_ref, active_ref, place_ref, *, peers, capacity
):
    place = places(got_ref, peers, capacity)
    place_ref[...] = place
    unpack(place, got_ref, small_ref, decoded_ref, active_ref, 1)


def unpack_first_kernel(got_ref, small_ref, place_ref, decoded_ref, active_ref):
    unpack(place_ref[...], got_ref, small_ref, decoded_ref, active_ref, 0)


def vertical(frame):
    wide = frame.astype(f32)
    y = iota(wide.shape, 0) % H
    up = jnp.where(y == 0, 0.0, pltpu.roll(wide, 1, 0))
    down = jnp.where(y == H - 1, 0.0, pltpu.roll(wide, wide.shape[0] - 1, 0))
    return up.astype(bf16), frame, down.astype(bf16)


def patches(frame):
    pixels, channels = frame.shape
    nothing = jnp.zeros((H, channels), bf16)
    parts = []
    for shifted in vertical(frame):
        parts.append(jnp.concatenate([nothing, shifted[: pixels - H]], 0))
        parts.append(shifted)
        parts.append(jnp.concatenate([shifted[H:], nothing], 0))
    return jnp.concatenate(parts, 1)


def kept(keep_ref):
    return [[keep_ref[3 * f + back : 3 * f + back + 1, :1] for back in range(3)] for f in range(2)]


def local_conv_kernel(
    keep_ref, first_ref, second_ref, here_ref, behind_ref, sum0_ref, sum1_ref
):
    keep = kept(keep_ref)
    channels = sum0_ref.shape[1]
    sum1 = convolve(patches(second_ref[...]), here_ref[...])
    both = mm(
        patches(first_ref[...]), jnp.concatenate([here_ref[...], behind_ref[...]], 1)
    )
    sum0_ref[...] = both[:, :channels]
    sum1_ref[...] = sum1 + keep[1][1] * both[:, channels:]


def second_residual_kernel(
    keep_ref, small_ref, prior_ref, far_ref, sum_ref, decoded_ref, out_ref, near_ref
):
    base = sum_ref[...] + decoded_ref[...].astype(f32) + small_ref[2:3, : out_ref.shape[1]]

    near = patches(prior_ref[...])
    near_ref[...] = near
    far = kept(keep_ref)[1][2] * convolve(near, far_ref[...])
    out_ref[...] = (base + far).astype(bf16)


def behind_kernel(
    keep_ref, small_ref, near_ref, behind_ref, sum_ref, decoded_ref, out_ref
):
    base = sum_ref[...] + decoded_ref[...].astype(f32) + small_ref[2:3, : out_ref.shape[1]]
    out_ref[...] = base + kept(keep_ref)[0][1] * convolve(near_ref[...], behind_ref[...])


def first_residual_kernel(keep_ref, prior_ref, far_ref, sum_ref, out_ref):
    far = kept(keep_ref)[0][2] * convolve(patches(prior_ref[...]), far_ref[...])
    out_ref[...] = (sum_ref[...] + far).astype(bf16)


def local_time_kernel(
    keep_ref, small_ref, first_ref, second_ref, time_ref, sum0_ref, sum1_ref
):
    keep = kept(keep_ref)
    bias = small_ref[3:4, : sum0_ref.shape[1]]
    sum0_ref[...] = mm(first_ref[...], time_ref[2]) + bias
    sum1_ref[...] = (
        mm(second_ref[...], time_ref[2]) + bias + keep[1][1] * mm(first_ref[...], time_ref[1])
    )


def upscale(temporal, frame, small_ref, folded_ref, made_ref, near, rows32):
    pixels = H * W
    channels = near.shape[1] // 3
    outs = folded_ref.shape[3]
    both = temporal.astype(bf16)
    nothing = jnp.zeros((H, 3 * channels), bf16)
    for half in range(2):
        base = H + half * (pixels + H)
        near[base - H : base] = nothing
        shown = both[:, half * channels : (half + 1) * channels]
        for a, shifted in enumerate(vertical(shown)):
            near[base : base + pixels, a * channels : (a + 1) * channels] = shifted
    near[2 * (H + pixels) :] = nothing
    span = 2 * pixels + H
    bias = small_ref[4:5, :outs]
    blocks = 2 * outs // 128
    for p in range(2):
        phases = []
        for q in range(2):
            windows = [
                near[
                    (q + side) * H : (q + side) * H + span, p * channels : (p + 2) * channels
                ]
                for side in range(2)
            ]
            phases.append(mm(jnp.concatenate(windows, 1), folded_ref[q, p]) + bias)
        pair = jnp.concatenate(phases, 1)
        for half in range(2):
            for x in range(W):
                row = half * (pixels + H) + x * H
                for block in range(blocks):
                    rows32[half, x * blocks + block, pl.ds(p, H, stride=2)] = pair[
                        row : row + H, block * 128 : (block + 1) * 128
                    ]
    for half in range(2):
        for block in range(W * blocks):
            made_ref[2 * frame + half, :, block * 128 : (block + 1) * 128] = rows32[
                half, block
            ].astype(bf16)


def early_up_kernel(
    keep_ref, small_ref, sum0_ref, sum1_ref, folded_ref, made_ref, near, rows32
):
    @pl.when(alone(keep_ref, 1))
    def _():
        upscale(sum1_ref[...], 1, small_ref, folded_ref, made_ref, near, rows32)

    @pl.when(alone(keep_ref, 0))
    def _():
        upscale(sum0_ref[...], 0, small_ref, folded_ref, made_ref, near, rows32)


def second_up_kernel(
    keep_ref, small_ref, prior_ref, time_ref, sum_ref, folded_ref, early_ref, made_ref,
    near, rows32,
):
    @pl.when(jnp.logical_not(alone(keep_ref, 1)))
    def _():
        temporal = sum_ref[...] + mm(prior_ref[...], time_ref[0])
        upscale(temporal, 1, small_ref, folded_ref, made_ref, near, rows32)


def first_up_kernel(
    keep_ref, small_ref, before_ref, prior_ref, time_ref, sum_ref, folded_ref, later_ref,
    out_hbm,
    made_ref, near, rows32, left,
):
    later = pltpu.make_async_copy(later_ref.at[2:4], out_hbm.at[2:4], left.at[0])
    later.start()
    lonely = alone(keep_ref, 0)

    @pl.when(lonely)
    def _():
        copy = pltpu.make_async_copy(later_ref.at[0:2], out_hbm.at[0:2], left.at[1])
        copy.start()
        copy.wait()

    @pl.when(jnp.logical_not(lonely))
    def _():
        seen = keep_ref[2:3, :1].astype(bf16)
        pair = jnp.concatenate([before_ref[...] * seen, prior_ref[...]], 1)
        both = time_ref[:2].reshape(pair.shape[1], time_ref.shape[2])
        temporal = sum_ref[...] + mm(pair, both)
        upscale(temporal, 0, small_ref, folded_ref, made_ref, near, rows32)
        copy = pltpu.make_async_copy(made_ref, out_hbm.at[0:2], left.at[1])
        copy.start()
        copy.wait()

    later.wait()


def keeps(counts_ref, position_ref):
    first = position_ref[0] * 2
    starts = [jnp.int32(0), jnp.int32(0)]
    end = jnp.int32(0)
    for video in range(counts_ref.shape[0]):
        end = end + counts_ref[video]
        starts = [jnp.where(end <= first + f, end, starts[f]) for f in range(2)]
    return [
        [(first + f - back >= starts[f]).astype(f32) for back in range(3)] for f in range(2)
    ]


def halves(taps):
    return (taps[0], taps[1] + taps[2]), (taps[0] + taps[1], taps[2])


def prepare_kernel(
    counts_ref, position_ref, gain_ref, shift_ref, res_bias_ref, time_bias_ref, up_bias_ref,
    up_hbm, taps_hbm,
    folded_ref, small_ref, keep_ref, here_ref, behind_hbm, far_hbm,
    up_ref, behind_ref, far_ref, arrived, left,
):
    copies = [
        pltpu.make_async_copy(up_hbm, up_ref, arrived.at[0]),
        pltpu.make_async_copy(taps_hbm.at[2], here_ref, arrived.at[1]),
        pltpu.make_async_copy(taps_hbm.at[1], behind_ref, arrived.at[2]),
        pltpu.make_async_copy(taps_hbm.at[0], far_ref, arrived.at[3]),
    ]
    for copy in copies:
        copy.start()
    small_ref[...] = jnp.zeros_like(small_ref)
    for i, ref in enumerate((gain_ref, shift_ref, res_bias_ref, time_bias_ref, up_bias_ref)):
        small_ref[i : i + 1, : ref.shape[1]] = ref[...]
    keep = keeps(counts_ref, position_ref)
    row = iota(keep_ref.shape, 0)
    seen = jnp.zeros(keep_ref.shape, f32)
    for f in range(2):
        for back in range(3):
            seen = jnp.where(row == 3 * f + back, keep[f][back], seen)
    keep_ref[...] = seen
    copies[0].wait()
    channels = up_ref.shape[3]
    columns = [
        halves([up_ref[a, b].astype(f32) for b in range(3)]) for a in range(3)
    ]
    for q in range(2):
        for side in range(2):
            rows = halves([columns[a][q][side] for a in range(3)])
            for p in range(2):
                for dy in range(2):
                    at = (2 * side + dy) * channels
                    folded_ref[q, p, at : at + channels] = rows[p][dy].T.astype(bf16)
    for copy in copies[1:]:
        copy.wait()
    sent = [
        pltpu.make_async_copy(behind_ref, behind_hbm, left.at[0]),
        pltpu.make_async_copy(far_ref, far_hbm, left.at[1]),
    ]
    for copy in sent:
        copy.start()
    for copy in sent:
        copy.wait()


def on_device(
    latent,
    owner,
    frame_counts,
    norm_gain,
    norm_shift,
    res_kernel,
    res_bias,
    time_kernel,
    time_bias,
    up_kernel,
    up_bias,
):
    peers = lax.axis_size("tm")
    position = lax.axis_index("tm").astype(jnp.int32).reshape(1)
    tokens, channels = latent.shape
    capacity = 2 * tokens // peers
    pixels = H * W
    wide = time_kernel.shape[-1]
    outs = up_kernel.shape[-1]

    packed = pl.pallas_call(
        functools.partial(pack_kernel, peers=peers, capacity=capacity),
        out_shape=jax.ShapeDtypeStruct((peers * capacity, channels), bf16),
        in_specs=[HB, HB],
        out_specs=HB,
        scratch_shapes=[
            pltpu.VMEM((1, tokens), jnp.int32),
            pltpu.VMEM((tokens, channels + 128), bf16),
            pltpu.VMEM((peers * capacity, channels), bf16),
            pltpu.SemaphoreType.DMA((2,)),
            pltpu.SemaphoreType.DMA((4,)),
        ],
        compiler_params=pltpu.CompilerParams(vmem_limit_bytes=16 * MIB),
        name="pack",
    )(in_hbm(owner.reshape(1, tokens)), in_hbm(latent))
    packed, up_kernel = lax.optimization_barrier((packed, up_kernel))
    received = lax.all_to_all(packed, "tm", split_axis=0, concat_axis=0, tiled=True)
    res_kernel = res_kernel.reshape(3, 9 * channels, channels)
    one_tap = (9 * channels, channels)
    res_kernel = in_hbm(res_kernel)
    folded, small, keep, here, behind, far = pl.pallas_call(
        prepare_kernel,
        out_shape=[
            jax.ShapeDtypeStruct((2, 2, 4 * channels, outs), bf16),
            pltpu.VMEM((8, wide), f32),
            pltpu.VMEM((8, 128), f32),
            pltpu.VMEM(one_tap, bf16),
            pltpu.HBM(one_tap, bf16),
            pltpu.HBM(one_tap, bf16),
        ],
        in_specs=[SM] * 2 + [VM] * 5 + [HB] * 2,
        out_specs=[VM] * 4 + [HB] * 2,
        scratch_shapes=[
            pltpu.VMEM((3, 3, outs, channels), bf16),
            pltpu.VMEM(one_tap, bf16),
            pltpu.VMEM(one_tap, bf16),
            pltpu.SemaphoreType.DMA((4,)),
            pltpu.SemaphoreType.DMA((2,)),
        ],
        compiler_params=pltpu.CompilerParams(vmem_limit_bytes=20 * MIB),
        cost_estimate=pl.CostEstimate(
            flops=0, bytes_accessed=2 * res_kernel.size * 2, transcendentals=0
        ),
        name="prepare",
    )(
        frame_counts,
        position,
        norm_gain.reshape(1, channels),
        norm_shift.reshape(1, channels),
        res_bias.reshape(1, channels),
        time_bias.reshape(1, wide),
        up_bias.reshape(1, outs),
        in_hbm(jnp.swapaxes(up_kernel, 2, 3)),
        res_kernel,
    )

    def call(body, name, outputs, arguments, scratch=(), share=1.0, **more):
        out_specs = more.pop("out_specs", [VM] * len(outputs))
        in_specs = more.pop("in_specs", [VM] * len(arguments))
        return pl.pallas_call(
            body,
            out_shape=outputs,
            in_specs=in_specs,
            out_specs=out_specs,
            scratch_shapes=scratch,
            compiler_params=pltpu.CompilerParams(vmem_limit_bytes=12 * MIB),
            cost_estimate=pl.CostEstimate(
                flops=int(share * tap), bytes_accessed=0, transcendentals=0
            ),
            name=name,
            **more,
        )(*arguments)

    vm = in_vmem
    frame16 = pltpu.VMEM((pixels, channels), bf16)
    frame32 = pltpu.VMEM((pixels, channels), f32)
    near_shape = pltpu.VMEM((pixels, 9 * channels), bf16)
    tap = 2 * pixels * 9 * channels * channels
    sem = pltpu.SemaphoreType.DMA
    small, keep, received = vm(small), vm(keep), vm(received)
    decoded1, active1, place = call(
        functools.partial(unpack_second_kernel, peers=peers, capacity=capacity),
        "unpack_second",
        [frame16] * 2 + [pltpu.VMEM((1, peers * capacity), jnp.int32)],
        [received, small],
        share=3,
    )
    prior1 = from_behind(active1, "tm")
    decoded0, active0 = call(
        unpack_first_kernel, "unpack_first", [frame16] * 2, [received, small, vm(place)], share=0
    )
    prior0 = from_behind(active0, "tm")
    behind, far = vm(behind), vm(far)
    sum0, sum1 = call(
        local_conv_kernel,
        "local_conv",
        [frame32] * 2,
        [keep, vm(active0), vm(active1), vm(here), behind],
        share=3,
    )
    second, near = call(
        second_residual_kernel,
        "second_residual",
        [frame16, near_shape],
        [keep, small, vm(prior1), far, vm(sum1), vm(decoded1)],
        share=1,
    )
    prior_second = from_behind(second, "tm")
    (sum0,) = call(
        behind_kernel,
        "behind",
        [frame32],
        [keep, small, vm(near), behind, vm(sum0), vm(decoded0)],
        share=1,
    )
    (first,) = call(
        first_residual_kernel,
        "first_residual",
        [frame16],
        [keep, vm(prior0), far, vm(sum0)],
        share=1,
    )
    prior_first = from_behind(first, "tm")
    times = vm(time_kernel)
    time0, time1 = call(
        local_time_kernel,
        "local_time",
        [pltpu.VMEM((pixels, wide), f32)] * 2,
        [keep, small, vm(first), vm(second), times],
        share=0.4,
    )
    frames = 2 * tokens // pixels
    shape = (frames, 2 * H, 2 * W * outs)
    up_scratch = [
        pltpu.VMEM((2 * pixels + 3 * H, 3 * channels), bf16),
        pltpu.VMEM((2, 2 * W * outs // 128, 2 * H, 128), f32),
    ]
    folded, prior_second = vm(folded), vm(prior_second)
    time0, time1 = vm(time0), vm(time1)
    (early,) = call(
        early_up_kernel,
        "early_up",
        [pltpu.VMEM(shape, bf16)],
        [keep, small, time0, time1, folded],
        up_scratch,
        share=2,
    )
    (later,) = call(
        second_up_kernel,
        "second_up",
        [pltpu.VMEM(shape, bf16)],
        [keep, small, prior_second, times, time1, folded, vm(early)],
        up_scratch,
        share=6,
        input_output_aliases={6: 0},
    )
    (made,) = call(
        first_up_kernel,
        "first_up",
        [jax.ShapeDtypeStruct(shape, bf16)],
        [keep, small, vm(prior_first), prior_second, times, time0, folded, vm(later)],
        [pltpu.VMEM((frames // 2,) + shape[1:], bf16)] + up_scratch + [sem((2,))],
        share=6,
        out_specs=[HB],
    )
    return made


def solution(mesh):
    placed = (
        P(("groups", "tm"), None),
        P(("groups", "tm")),
        P("groups"),
        P(),
        P(),
        P(),
        P(),
        P(),
        P(),
        P(),
        P(),
    )
    return jax.shard_map(
        on_device,
        mesh=mesh,
        in_specs=placed,
        out_specs=P(("groups", "tm"), None, None),
        check_vma=False,
    )
```

time: 54.4 us -> 50.1 us (0.921)
  waiting for transfers between devices: 19.7 us -> 15.4 us
  starting transfers between devices: 9.6 us -> 8.84 us
    all_to_all x1, waiting for transfers between devices: 14.1 us -> 10.3 us  [on_device(): lax.all_to_all(packed, 'tm', split_axis=0, concat_axis=0, tiled=True)]
    pallas_call x1, Pallas kernels: 2.86 us -> 6.68 us  [on_device(): pl.pallas_call(prepare_kernel, out_shape=[jax.ShapeDtypeStruct((2, 2, 4 *...]
    pallas_call x9 -> x10, Pallas kernels: 17.3 us -> 13.8 us  [call(): pl.pallas_call(body, out_shape=outputs, in_specs=in_specs, out_specs=out_...]
    ppermute x4, starting transfers between devices: 2.2 us -> 1.45 us  [from_behind(): return lax.ppermute(value, axis, [(i, (i + 1) % size) for i in range(size)])]
    unnamed x14 -> x22, local copies, waits for them, and re-layouts: 1.66 us -> 2.18 us
  transfers between devices with their start and end apart: 5 -> 5, of which waited for: 3 -> 3; matrix products, arithmetic and copies ran while one was open for 0% -> 0% of each run, Pallas kernels for 28% -> 37%
where the time goes in v2:
time: 50.1 us; the launch traced here: 49.9 us
  Pallas kernels  23 us (46%)
  waiting for transfers between devices  15.4 us (31%)
  starting transfers between devices  8.84 us (18%)
  local copies, waits for them, and re-layouts  2.19 us (4%)
    pallas_call x10, Pallas kernels, call(): pl.pallas_call(body, out_shape=outputs, in_specs=in_specs, out_specs=out_...  13.8 us
    all_to_all x1, waiting for transfers between devices, on_device(): lax.all_to_all(packed, 'tm', split_axis=0, concat_axis=0, tiled=True)  10.3 us
    all_to_all x1, starting transfers between devices, on_device(): lax.all_to_all(packed, 'tm', split_axis=0, concat_axis=0, tiled=True)  7.4 us
    pallas_call x1, Pallas kernels, on_device(): pl.pallas_call(prepare_kernel, out_shape=[jax.ShapeDtypeStruct((2, 2, 4 *...  6.68 us
    ppermute x4, waiting for transfers between devices, from_behind(): return lax.ppermute(value, axis, [(i, (i + 1) % size) for i in range(size)])  5.13 us
    pallas_call x1, Pallas kernels, on_device(): pl.pallas_call(functools.partial(pack_kernel, peers=peers, capacity=capac...  2.54 us
    unnamed x22, local copies, waits for them, and re-layouts  2.18 us
    ppermute x4, starting transfers between devices, from_behind(): return lax.ppermute(value, axis, [(i, (i + 1) % size) for i in range(size)])  1.45 us
  transfers between devices with their start and end apart: 5, of which 3 were waited for; matrix products, arithmetic and copies ran while one was open for 0% of the time, Pallas kernels for 37%

profile of v2, /device:TPU:0, one launch (start us, length us, event | category | flops | bytes accessed | tf_op | source)
XLA Modules:
  0.0 49.9 jit_solution(8630158528556746729)
XLA Ops:
  0.0 0.0 copy-start.6
  0.0 2.5 %pack.1 = bf16[1024,384]{1,0:T(8,128)(2,1)} custom-call(s32[1,512]{1,0:T(1,128)} %bitcast.12, bf16[512,384]{1,0:T(8,128)(2,1)} %latent_hbm.1), custom_call_target="tpu_custom_call" | custom-call | tf_op jit(solution)/shard_map/pack/pallas_call | solution.py:377
  2.6 7.4 %all-to-all-start = ((bf16[16,64,384]{2,1,0:T(8,128)(2,1)}), bf16[16,64,384]{2,1,0:T(8,128)(2,1)S(1)}, u32[]{:S(2)}, u32[]{:S(2)}) async-start(bf16[16,64,384]{2,1,0:T(8,128)(2,1)} %bitcast.5), calls=%async_computation | async-start | bytes 1572864 | tf_op jit(solution)/shard_map/all_to_all | solution.py:393
  10.0 0.0 copy-done.8
  10.0 0.0 copy-done.9
  10.0 0.0 copy-done.10
  10.0 0.0 copy-done.7
  10.1 6.7 %prepare.1 = (bf16[2,2,1536,192]{3,2,1,0:T(8,128)(2,1)S(1)}, f32[8,768]{1,0:T(8,128)S(1)}, f32[8,128]{1,0:T(8,128)S(1)}, bf16[3456,384]{1,0:T(8,128)(2,1)S(1)}, ...) custom-call(s32[8]{0:T(128)S(1)} %copy-done.6, s32[1]{0:T(128)} %bitcast.position_ref, ...), custom_call_target="tpu_custom_call" | custom-call | bytes 15925248 | tf_op jit(solution)/shard_map/prepare/pallas_call | solution.py:397
  16.8 0.0 copy-start.1
  16.8 1.6 %copy-done.1 = bf16[2,2,1536,192]{3,2,1,0:T(8,128)(2,1)} copy-done((bf16[2,2,1536,192]{3,2,1,0:T(8,128)(2,1)}, bf16[2,2,1536,192]{3,2,1,0:T(8,128)(2,1)S(1)}, u32[]{:S(2)}) %copy-start.1) | copy-done | bytes 2359320
  18.4 10.3 %all-to-all-done = bf16[16,64,384]{2,1,0:T(8,128)(2,1)S(1)} async-done(((bf16[16,64,384]{2,1,0:T(8,128)(2,1)}), bf16[16,64,384]{2,1,0:T(8,128)(2,1)S(1)}, u32[]{:S(2)}, u32[]{:S(2)}) %all-to-all-start) | async-done | bytes 786464 | tf_op jit(solution)/shard_map/all_to_all | solution.py:393
  28.7 0.9 %unpack_second.1 = (bf16[256,384]{1,0:T(8,128)(2,1)S(1)}, bf16[256,384]{1,0:T(8,128)(2,1)S(1)}, s32[1,1024]{1,0:T(1,128)S(1)}) custom-call(bf16[1024,384]{1,0:T(8,128)(2,1)S(1)} %bitcast.7, f32[8,768]{1,0:T(8,128)S(1)} %get-tuple-element.26.small_ref), custom_call_target="tpu_custom_call" | custom-call | flops 2038431744 | tf_op jit(solution)/shard_map/unpack_second/pallas_call | solution.py:436
  29.6 0.3 collective-permute-start.1
  29.9 0.6 %unpack_first.1 = (bf16[256,384]{1,0:T(8,128)(2,1)S(1)}, bf16[256,384]{1,0:T(8,128)(2,1)S(1)}) custom-call(bf16[1024,384]{1,0:T(8,128)(2,1)S(1)} %bitcast.8, f32[8,768]{1,0:T(8,128)S(1)} %get-tuple-element.26.small_ref, s32[1,1024]{1,0:T(1,128)S(1)} %get-tuple-element.28.place_ref), custom_call_target="tpu_custom_call" | custom-call | tf_op jit(solution)/shard_map/unpack_first/pallas_call | solution.py:436
  30.5 1.0 %collective-permute-start = (bf16[256,384]{1,0:T(8,128)(2,1)S(1)}, bf16[256,384]{1,0:T(8,128)(2,1)S(1)}, u32[]{:S(2)}, u32[]{:S(2)}) collective-permute-start(bf16[256,384]{1,0:T(8,128)(2,1)S(1)} %get-tuple-element.29.first_ref), channel_id=1, source_target_pairs={{0,1},{1,2},{2,3},{3,4},{4,5},{5,6},{6,7},{7,8},{8,9},{9,10},{10,1... | collective-permute-start | bytes 589832 | tf_op jit(solution)/shard_map/ppermute | solution.py:51
  31.6 2.4 %local_conv.1 = (f32[256,384]{1,0:T(8,128)S(1)}, f32[256,384]{1,0:T(8,128)S(1)}) custom-call(f32[8,128]{1,0:T(8,128)S(1)} %get-tuple-element.25.keep_ref, bf16[256,384]{1,0:T(8,128)(2,1)S(1)} %get-tuple-element.29.first_ref, bf16[256,384]{1,0:T(8,128)(2,1)S(1)} %get-tuple-element.31.second_ref, bf16[3456,384]{1,0:T(8,128)(2,1)S(1)} %get-tuple-element.32.here_ref, ...), custom_call_target="tpu_custom_call" | custom-call | flops 2038431744 | tf_op jit(solution)/shard_map/local_conv/pallas_call | solution.py:436
  34.0 3.5 %collective-permute-done.1.prior_ref = bf16[256,384]{1,0:T(8,128)(2,1)S(1)} collective-permute-done((bf16[256,384]{1,0:T(8,128)(2,1)S(1)}, bf16[256,384]{1,0:T(8,128)(2,1)S(1)}, u32[]{:S(2)}, u32[]{:S(2)}) %collective-permute-start.1) | collective-permute-done | bytes 196640 | tf_op jit(solution)/shard_map/ppermute | solution.py:51
  37.4 1.1 %second_residual.1 = (bf16[256,384]{1,0:T(8,128)(2,1)S(1)}, bf16[256,3456]{1,0:T(8,128)(2,1)S(1)}) custom-call(f32[8,128]{1,0:T(8,128)S(1)} %get-tuple-element.25.keep_ref, f32[8,768]{1,0:T(8,128)S(1)} %get-tuple-element.26.small_ref, bf16[256,384]{1,0:T(8,128)(2,1)S(1)} %collective-permute-done.1.prior_ref, bf16[3456,384]{1,0:T(8,128)(2,1)S(1)} %copy-done, ...), custom_call_target="tpu_custom_call" | custom-call | flops 679477248 | tf_op jit(solution)/shard_map/second_residual/pallas_call | solution.py:436
  38.6 0.1 collective-permute-start.3
  38.6 1.0 %behind.1.sum_ref = f32[256,384]{1,0:T(8,128)S(1)} custom-call(f32[8,128]{1,0:T(8,128)S(1)} %get-tuple-element.25.keep_ref, f32[8,768]{1,0:T(8,128)S(1)} %get-tuple-element.26.small_ref, bf16[256,3456]{1,0:T(8,128)(2,1)S(1)} %get-tuple-element.36.near_ref, bf16[3456,384]{1,0:T(8,128)(2,1)S(1)} %copy-done.3, f32[256,384]{1,0:T(8,128)S(1)} %get-tuple-element.37.sum_ref, ...), custom_call_target="tpu_custom_call" | custom-call | flops 679477248 | tf_op jit(solution)/shard_map/behind/pallas_call | solution.py:436
  39.7 0.0 copy-start.4
  39.7 0.0 collective-permute-done.prior_ref
  39.7 1.0 %first_residual.1.first_ref = bf16[256,384]{1,0:T(8,128)(2,1)S(1)} custom-call(f32[8,128]{1,0:T(8,128)S(1)} %get-tuple-element.25.keep_ref, bf16[256,384]{1,0:T(8,128)(2,1)S(1)} %collective-permute-done.prior_ref, bf16[3456,384]{1,0:T(8,128)(2,1)S(1)} %copy-done, f32[256,384]{1,0:T(8,128)S(1)} %behind.1.sum_ref), custom_call_target="tpu_custom_call" | custom-call | flops 679477248 | tf_op jit(solution)/shard_map/first_residual/pallas_call | solution.py:436
  40.7 0.1 collective-permute-start.2
  40.8 0.4 copy-done.4
  41.2 0.8 %local_time.1 = (f32[256,768]{1,0:T(8,128)S(1)}, f32[256,768]{1,0:T(8,128)S(1)}) custom-call(f32[8,128]{1,0:T(8,128)S(1)} %get-tuple-element.25.keep_ref, f32[8,768]{1,0:T(8,128)S(1)} %get-tuple-element.26.small_ref, bf16[256,384]{1,0:T(8,128)(2,1)S(1)} %first_residual.1.first_ref, bf16[256,384]{1,0:T(8,128)(2,1)S(1)} %get-tuple-element.39.second_ref, ...), custom_call_target="tpu_custom_call" | custom-call | flops 271790912 | tf_op jit(solution)/shard_map/local_time/pallas_call | solution.py:436
  42.0 0.2 copy-done.2
  42.1 4.7 %early_up.1.early_ref = bf16[4,32,6144]{2,1,0:T(8,128)(2,1)S(1)} custom-call(f32[8,128]{1,0:T(8,128)S(1)} %get-tuple-element.25.keep_ref, f32[8,768]{1,0:T(8,128)S(1)} %get-tuple-element.26.small_ref, f32[256,768]{1,0:T(8,128)S(1)} %get-tuple-element.40.sum0_ref.sum_ref, f32[256,768]{1,0:T(8,128)S(1)} %get-tuple-element.42.sum1_ref.sum_ref, ...), custom_call_target="tpu_custom_call" | custom-call | flops 1358954496 | tf_op jit(solution)/shard_map/early_up/pallas_call | solution.py:436
  46.8 0.0 collective-permute-done.3.prior_ref
  46.8 0.1 second_up.1.later_ref
  46.9 1.6 %collective-permute-done.2.before_ref = bf16[256,384]{1,0:T(8,128)(2,1)S(1)} collective-permute-done((bf16[256,384]{1,0:T(8,128)(2,1)S(1)}, bf16[256,384]{1,0:T(8,128)(2,1)S(1)}, u32[]{:S(2)}, u32[]{:S(2)}) %collective-permute-start.2) | collective-permute-done | bytes 196640 | tf_op jit(solution)/shard_map/ppermute | solution.py:51
  48.6 1.2 %first_up.1 = bf16[4,32,6144]{2,1,0:T(8,128)(2,1)} custom-call(f32[8,128]{1,0:T(8,128)S(1)} %get-tuple-element.25.keep_ref, f32[8,768]{1,0:T(8,128)S(1)} %get-tuple-element.26.small_ref, bf16[256,384]{1,0:T(8,128)(2,1)S(1)} %collective-permute-done.2.before_ref, bf16[256,384]{1,0:T(8,128)(2,1)S(1)} %collective-permute-done.3.prior_ref, ...), custom_call_target="tpu_custom_call" | custom-call | flops 4076863488 | tf_op jit(solution)/shard_map/first_up/pallas_call | solution.py:436
  (16 shorter events, 0.0 us)
Async XLA Ops:
  0.0 10.0 %copy-start.8 = (f32[384]{0:T(512)S(1)}, f32[384]{0:T(512)}, u32[]{:S(2)}) copy-start(f32[384]{0:T(512)} %param.14) | copy-start | bytes 4612
  0.0 10.0 %copy-start.9 = (f32[384]{0:T(512)S(1)}, f32[384]{0:T(512)}, u32[]{:S(2)}) copy-start(f32[384]{0:T(512)} %param.15) | copy-start | bytes 4612
  0.0 10.0 %copy-start.10 = (f32[384]{0:T(512)S(1)}, f32[384]{0:T(512)}, u32[]{:S(2)}) copy-start(f32[384]{0:T(512)} %param.17) | copy-start | bytes 4612
  0.0 10.0 %copy-start.7 = (f32[768]{0:T(1024)S(1)}, f32[768]{0:T(1024)}, u32[]{:S(2)}) copy-start(f32[768]{0:T(1024)} %param.19) | copy-start | bytes 9220
  0.0 10.1 %copy-start.5 = (f32[192]{0:T(256)S(1)}, f32[192]{0:T(256)}, u32[]{:S(2)}) copy-start(f32[192]{0:T(256)} %param.21) | copy-start | bytes 2308
  0.0 10.1 %copy-start.6 = (s32[8]{0:T(128)S(1)}, s32[8]{0:T(128)}, u32[]{:S(2)}) copy-start(s32[8]{0:T(128)} %counts_ref.1) | copy-start | bytes 100
  2.6 26.1 %all-to-all-start = ((bf16[16,64,384]{2,1,0:T(8,128)(2,1)}), bf16[16,64,384]{2,1,0:T(8,128)(2,1)S(1)}, u32[]{:S(2)}, u32[]{:S(2)}) async-start(bf16[16,64,384]{2,1,0:T(8,128)(2,1)} %bitcast.5), calls=%async_computation | async-start | bytes 1572864 | tf_op jit(solution)/shard_map/all_to_all | solution.py:393
  16.8 1.6 %copy-start.1 = (bf16[2,2,1536,192]{3,2,1,0:T(8,128)(2,1)}, bf16[2,2,1536,192]{3,2,1,0:T(8,128)(2,1)S(1)}, u32[]{:S(2)}) copy-start(bf16[2,2,1536,192]{3,2,1,0:T(8,128)(2,1)S(1)} %get-tuple-element.41.folded_ref) | copy-start | bytes 7077892
  28.7 2.9 %copy-start.3 = (bf16[3456,384]{1,0:T(8,128)(2,1)S(1)}, bf16[3456,384]{1,0:T(8,128)(2,1)}, u32[]{:S(2)}) copy-start(bf16[3456,384]{1,0:T(8,128)(2,1)} %get-tuple-element.33.behind_ref) | copy-start | bytes 7962628
  29.6 7.8 %collective-permute-start.1 = (bf16[256,384]{1,0:T(8,128)(2,1)S(1)}, bf16[256,384]{1,0:T(8,128)(2,1)S(1)}, u32[]{:S(2)}, u32[]{:S(2)}) collective-permute-start(bf16[256,384]{1,0:T(8,128)(2,1)S(1)} %get-tuple-element.31.second_ref), channel_id=1, source_target_pairs={{0,1},{1,2},{2,3},{3,4},{4,5},{5,6},{6,7},{7,8},{8,9},{9,10},{10,1... | collective-permute-start | bytes 589832 | tf_op jit(solution)/shard_map/ppermute | solution.py:51
  30.5 9.1 %collective-permute-start = (bf16[256,384]{1,0:T(8,128)(2,1)S(1)}, bf16[256,384]{1,0:T(8,128)(2,1)S(1)}, u32[]{:S(2)}, u32[]{:S(2)}) collective-permute-start(bf16[256,384]{1,0:T(8,128)(2,1)S(1)} %get-tuple-element.29.first_ref), channel_id=1, source_target_pairs={{0,1},{1,2},{2,3},{3,4},{4,5},{5,6},{6,7},{7,8},{8,9},{9,10},{10,1... | collective-permute-start | bytes 589832 | tf_op jit(solution)/shard_map/ppermute | solution.py:51
  31.6 5.9 %copy-start = (bf16[3456,384]{1,0:T(8,128)(2,1)S(1)}, bf16[3456,384]{1,0:T(8,128)(2,1)}, u32[]{:S(2)}) copy-start(bf16[3456,384]{1,0:T(8,128)(2,1)} %get-tuple-element.30.far_ref) | copy-start | bytes 7962628
  38.6 8.2 %collective-permute-start.3 = (bf16[256,384]{1,0:T(8,128)(2,1)S(1)}, bf16[256,384]{1,0:T(8,128)(2,1)S(1)}, u32[]{:S(2)}, u32[]{:S(2)}) collective-permute-start(bf16[256,384]{1,0:T(8,128)(2,1)S(1)} %get-tuple-element.39.second_ref), channel_id=1, source_target_pairs={{0,1},{1,2},{2,3},{3,4},{4,5},{5,6},{6,7},{7,8},{8,9},{9,10},{10,1... | collective-permute-start | bytes 589832 | tf_op jit(solution)/shard_map/ppermute | solution.py:51
  39.7 1.5 %copy-start.4 = (bf16[3,384,768]{2,1,0:T(8,128)(2,1)S(1)}, bf16[3,384,768]{2,1,0:T(8,128)(2,1)}, u32[]{:S(2)}) copy-start(bf16[3,384,768]{2,1,0:T(8,128)(2,1)} %time_ref.5) | copy-start | bytes 5308420
  39.7 2.4 %copy-start.2 = (bf16[2,2,1536,192]{3,2,1,0:T(8,128)(2,1)S(1)}, bf16[2,2,1536,192]{3,2,1,0:T(8,128)(2,1)}, u32[]{:S(2)}) copy-start(bf16[2,2,1536,192]{3,2,1,0:T(8,128)(2,1)} %copy-done.1) | copy-start | bytes 7077892
  40.7 7.8 %collective-permute-start.2 = (bf16[256,384]{1,0:T(8,128)(2,1)S(1)}, bf16[256,384]{1,0:T(8,128)(2,1)S(1)}, u32[]{:S(2)}, u32[]{:S(2)}) collective-permute-start(bf16[256,384]{1,0:T(8,128)(2,1)S(1)} %first_residual.1.first_ref), channel_id=1, source_target_pairs={{0,1},{1,2},{2,3},{3,4},{4,5},{5,6},{6,7},{7,8},{8,9},{9,10},{10,1... | collective-permute-start | bytes 589832 | tf_op jit(solution)/shard_map/ppermute | solution.py:51
